TPU v7x, 32 devices: a whole 2x2x4 slice. The times are simulated.
32 devices in a mesh: dp: 4 (over z), row: 2 (over x), col: 4 (over y, core).
Axes of the slice: x: 2, y: 2, z: 4, core: 2. Of those that a mesh axis runs over, the one named last changes fastest.
Arguments:
- tokens: bfloat16 [4096, 1024], P('dp', ('col', 'row'))
- segment_ids: int32 [4096], P('dp'), may hold values from 0 to 15, never falling along the last dimension, each value on 1 to 2048 neighbouring positions
- out_grad: bfloat16 [4096, 1024], P('dp', ('col', 'row')), may hold values from -6 to 6
- qkv_weight: float32 [1024, 16, 3, 64], P(('col', 'dp'), 'row'), may hold values from -0.1875 to 0.1875
- qkv_first: float32 [1024, 16, 3, 64], P(('col', 'dp'), 'row')
- qkv_second: float32 [1024, 16, 3, 64], P(('col', 'dp'), 'row')
- out_weight: float32 [1024, 1024], P(('row', 'dp'), 'col'), may hold values from -1.5 to 1.5
- out_first: float32 [1024, 1024], P(('row', 'dp'), 'col')
- out_second: float32 [1024, 1024], P(('row', 'dp'), 'col')
- up_weight: float32 [1024, 4096], P('col', ('row', 'dp')), may hold values from -0.1875 to 0.1875
- up_first: float32 [1024, 4096], P('col', ('row', 'dp'))
- up_second: float32 [1024, 4096], P('col', ('row', 'dp'))
- down_weight: float32 [4096, 1024], P(('row', 'dp'), 'col'), may hold values from -0.09375 to 0.09375
- down_first: float32 [4096, 1024], P(('row', 'dp'), 'col')
- down_second: float32 [4096, 1024], P(('row', 'dp'), 'col')
- qkv_bias: float32 [16, 192], P(('row', 'col'), 'dp'), may hold values from -1.5 to 1.5
- qkv_bias_first: float32 [16, 192], P(('row', 'col'), 'dp')
- qkv_bias_second: float32 [16, 192], P(('row', 'col'), 'dp')
- up_bias: float32 [4096], P(('row', 'col', 'dp')), may hold values from -1.5 to 1.5
- up_bias_first: float32 [4096], P(('row', 'col', 'dp'))
- up_bias_second: float32 [4096], P(('row', 'col', 'dp'))
- norm_vectors: float32 [6, 1024], P(None, ('col', 'row', 'dp'))
- norm_first: float32 [6, 1024], P(None, ('col', 'row', 'dp'))
- norm_second: float32 [6, 1024], P(None, ('col', 'row', 'dp'))
Outputs:
- block_out: bfloat16 [4096, 1024], P('dp', ('col', 'row'))
- input_grad: float32 [4096, 1024], P('dp', ('col', 'row'))
- new_qkv_weight: float32 [1024, 16, 3, 64], P(('col', 'dp'), 'row')
- new_qkv_first: float32 [1024, 16, 3, 64], P(('col', 'dp'), 'row')
- new_qkv_second: float32 [1024, 16, 3, 64], P(('col', 'dp'), 'row')
- new_out_weight: float32 [1024, 1024], P(('row', 'dp'), 'col')
- new_out_first: float32 [1024, 1024], P(('row', 'dp'), 'col')
- new_out_second: float32 [1024, 1024], P(('row', 'dp'), 'col')
- new_up_weight: float32 [1024, 4096], P('col', ('row', 'dp'))
- new_up_first: float32 [1024, 4096], P('col', ('row', 'dp'))
- new_up_second: float32 [1024, 4096], P('col', ('row', 'dp'))
- new_down_weight: float32 [4096, 1024], P(('row', 'dp'), 'col')
- new_down_first: float32 [4096, 1024], P(('row', 'dp'), 'col')
- new_down_second: float32 [4096, 1024], P(('row', 'dp'), 'col')
- new_qkv_bias: float32 [16, 192], P(('row', 'col'), 'dp')
- new_qkv_bias_first: float32 [16, 192], P(('row', 'col'), 'dp')
- new_qkv_bias_second: float32 [16, 192], P(('row', 'col'), 'dp')
- new_up_bias: float32 [4096], P(('row', 'col', 'dp'))
- new_up_bias_first: float32 [4096], P(('row', 'col', 'dp'))
- new_up_bias_second: float32 [4096], P(('row', 'col', 'dp'))
- new_norm_vectors: float32 [6, 1024], P(None, ('col', 'row', 'dp'))
- new_norm_first: float32 [6, 1024], P(None, ('col', 'row', 'dp'))
- new_norm_second: float32 [6, 1024], P(None, ('col', 'row', 'dp'))
Inputs may be any that keep to these rules, and one draw needn't show every extreme that they name: `segment_ids`: ids never fall along the tokens; each id covers 1 to 2048 consecutive tokens and one covers exactly 2048.
All inputs are finite; a program needn't handle non-finite values.
Results may differ from a plain program's by a relative error of at most 0.02.
Values may be sent and summed in bfloat16 or wider, within the bound.
A program may use at most 128 MiB of HBM per device.

v0:
```python
import math

import jax
import jax.numpy as jnp
from jax import lax
from jax.sharding import PartitionSpec as P

D = 1024
HD = 64
SEQ = 512
STEP = 10


EPS_NORM = 1e-05
BETA_ONE = 0.9
BETA_TWO = 0.999
EPS_ADAM = 1e-08
NEG_FILL = -1000000000.0
RATES = (0.05, 0.4, 0.05, 0.05, 0.3, 0.3, 0.5)
DECAYS = (0.01, 0.01, 0.01, 0.01, 0.0, 0.0, 0.0)


def gather_rows(shard_block):
    return lax.all_gather(shard_block, "row", axis=1, tiled=True)


def scatter_rows(partial_terms):
    return lax.psum_scatter(partial_terms, "row", scatter_dimension=1, tiled=True)


def gather_cols(shard_block):
    return lax.all_gather(shard_block, "col", axis=1, tiled=True)


def scatter_cols(partial_terms):
    return lax.psum_scatter(partial_terms, "col", scatter_dimension=1, tiled=True)


def feature_sums(first_term, second_term):
    return lax.psum((first_term, second_term), ("row", "col"))


def contract_rows(left_side, right_side):
    return lax.dot_general(
        left_side, right_side, (((0,), (0,)), ((), ())), preferred_element_type=jnp.float32
    )


def contract_cols(left_side, right_side):
    return lax.dot_general(
        left_side, right_side, (((1,), (1,)), ((), ())), preferred_element_type=jnp.float32
    )


def gelu_exact(values_in):
    return jax.nn.gelu(values_in, approximate=False)


def norm_forward(residual, norm_gain, norm_shift):
    sum_first, sum_second = feature_sums(
        jnp.sum(residual, axis=1, keepdims=True),
        jnp.sum(residual * residual, axis=1, keepdims=True),
    )
    mean_row = sum_first / D
    scale_row = lax.rsqrt(sum_second / D - mean_row * mean_row + EPS_NORM)
    normed = (residual - mean_row) * scale_row
    return (normed * norm_gain + norm_shift, normed, scale_row)


def norm_backward(grad_out, norm_gain, normed, scale_row):
    grad_normed = grad_out * norm_gain
    sum_plain, sum_cross = feature_sums(
        jnp.sum(grad_normed, axis=1, keepdims=True),
        jnp.sum(grad_normed * normed, axis=1, keepdims=True),
    )
    grad_resid = scale_row * (grad_normed - sum_plain / D - normed * (sum_cross / D))
    return (grad_resid, jnp.sum(grad_out * normed, axis=0), jnp.sum(grad_out, axis=0))


def masked_scores(queries, key_rows, same_doc):
    raw_scores = jnp.einsum(
        "sqhd,skhd->shqk", queries, key_rows, preferred_element_type=jnp.float32
    ) * (1.0 / math.sqrt(HD))
    return jnp.where(same_doc, raw_scores, NEG_FILL)


def shards(
    tokens,
    segment_ids,
    out_grad,
    qkv_weight,
    qkv_first,
    qkv_second,
    out_weight,
    out_first,
    out_second,
    up_weight,
    up_first,
    up_second,
    down_weight,
    down_first,
    down_second,
    qkv_bias,
    qkv_bias_first,
    qkv_bias_second,
    up_bias,
    up_bias_first,
    up_bias_second,
    norm_vectors,
    norm_first,
    norm_second,
):
    masters = (qkv_weight, out_weight, up_weight, down_weight, qkv_bias, up_bias, norm_vectors)
    firsts = (qkv_first, out_first, up_first, down_first, qkv_bias_first, up_bias_first, norm_first)
    seconds = (
        qkv_second,
        out_second,
        up_second,
        down_second,
        qkv_bias_second,
        up_bias_second,
        norm_second,
    )
    bf16 = jnp.bfloat16
    f32 = jnp.float32
    w_qkv, w_out, w_up, w_down, b_qkv, b_up, vectors = (
        lax.all_gather(qkv_weight.astype(bf16), "dp", axis=0, tiled=True),
        lax.all_gather(out_weight.astype(bf16), "dp", axis=0, tiled=True),
        lax.all_gather(up_weight.astype(bf16), "dp", axis=1, tiled=True),
        lax.all_gather(down_weight.astype(bf16), "dp", axis=0, tiled=True),
        lax.all_gather(qkv_bias.astype(bf16), "dp", axis=1, tiled=True),
        lax.all_gather(up_bias.astype(bf16), "dp", axis=0, tiled=True),
        lax.all_gather(norm_vectors.astype(bf16), "dp", axis=1, tiled=True),
    )
    vector_rows = vectors.astype(f32)
    tok_count = tokens.shape[0]
    seq_count = tok_count // SEQ
    heads_local = b_qkv.shape[0]
    score_scale = 1.0 / math.sqrt(HD)
    qkv_matrix = w_qkv.reshape(w_qkv.shape[0], -1)
    seg_rows = segment_ids.reshape(seq_count, SEQ)
    same_doc = seg_rows[:, None, :, None] == seg_rows[:, None, None, :]
    token_rows = gather_rows(tokens)
    qkv_local = scatter_cols(
        jnp.dot(token_rows, qkv_matrix, preferred_element_type=f32)
    ) + b_qkv.astype(f32).reshape(-1)
    qkv_low = qkv_local.astype(bf16).reshape(seq_count, SEQ, heads_local, 3, HD)
    queries = qkv_low[:, :, :, 0]
    key_rows = qkv_low[:, :, :, 1]
    value_rows = qkv_low[:, :, :, 2]
    scores = masked_scores(queries, key_rows, same_doc)
    row_peak = jnp.max(scores, axis=-1, keepdims=True)
    exp_scores = jnp.exp(scores - row_peak)
    row_total = jnp.sum(exp_scores, axis=-1, keepdims=True)
    log_total = row_peak + jnp.log(row_total)
    soft_low = (exp_scores / row_total).astype(bf16)
    attended = jnp.einsum("shqk,skhd->sqhd", soft_low, value_rows, preferred_element_type=f32)
    attended_rows = gather_cols(attended.reshape(tok_count, heads_local * HD).astype(bf16))
    residual_one = (
        tokens.astype(f32)
        + scatter_rows(jnp.dot(attended_rows, w_out, preferred_element_type=f32))
        + vector_rows[0]
    )
    hidden_one, normed_one, scale_one = norm_forward(residual_one, vector_rows[1], vector_rows[2])
    hidden_rows = gather_rows(hidden_one.astype(bf16))
    pre_act = scatter_cols(jnp.dot(hidden_rows, w_up, preferred_element_type=f32)) + b_up.astype(
        f32
    )
    act_rows = gather_cols(gelu_exact(pre_act).astype(bf16))
    residual_two = (
        hidden_one
        + scatter_rows(jnp.dot(act_rows, w_down, preferred_element_type=f32))
        + vector_rows[3]
    )
    output_rows, normed_two, scale_two = norm_forward(residual_two, vector_rows[4], vector_rows[5])
    block_out = output_rows.astype(bf16)
    grad_two, grad_gain_two, grad_shift_two = norm_backward(
        out_grad.astype(f32), vector_rows[4], normed_two, scale_two
    )
    grad_down_bias = jnp.sum(grad_two, axis=0)
    grad_two_rows = gather_rows(grad_two.astype(bf16))
    grad_down = contract_rows(act_rows, grad_two_rows)
    grad_act = scatter_cols(contract_cols(grad_two_rows, w_down))
    gelu_value, gelu_pull = jax.vjp(gelu_exact, pre_act)
    grad_pre = gelu_pull(grad_act)[0]
    grad_up_bias = jnp.sum(grad_pre, axis=0)
    grad_pre_rows = gather_cols(grad_pre.astype(bf16))
    grad_up = contract_rows(hidden_rows, grad_pre_rows)
    grad_hidden = grad_two + scatter_rows(contract_cols(grad_pre_rows, w_up))
    grad_one, grad_gain_one, grad_shift_one = norm_backward(
        grad_hidden, vector_rows[1], normed_one, scale_one
    )
    grad_out_bias = jnp.sum(grad_one, axis=0)
    grad_one_rows = gather_rows(grad_one.astype(bf16))
    grad_out = contract_rows(attended_rows, grad_one_rows)
    grad_att = scatter_cols(contract_cols(grad_one_rows, w_out))
    grad_att_low = grad_att.astype(bf16).reshape(seq_count, SEQ, heads_local, HD)
    soft_again = jnp.exp(scores - log_total)
    grad_soft = jnp.einsum("sqhd,skhd->shqk", grad_att_low, value_rows, preferred_element_type=f32)
    grad_values = jnp.einsum(
        "shqk,sqhd->skhd", soft_again.astype(bf16), grad_att_low, preferred_element_type=f32
    )
    row_dot = jnp.sum(soft_again * grad_soft, axis=-1, keepdims=True)
    grad_scores = (soft_again * (grad_soft - row_dot)).astype(bf16)
    grad_queries = (
        jnp.einsum("shqk,skhd->sqhd", grad_scores, key_rows, preferred_element_type=f32)
        * score_scale
    )
    grad_keys = (
        jnp.einsum("shqk,sqhd->skhd", grad_scores, queries, preferred_element_type=f32)
        * score_scale
    )
    grad_qkv = jnp.stack((grad_queries, grad_keys, grad_values), axis=3).reshape(tok_count, -1)
    grad_qkv_bias = jnp.sum(grad_qkv, axis=0).reshape(b_qkv.shape)
    grad_qkv_rows = gather_cols(grad_qkv.astype(bf16))
    grad_qkv_weight = contract_rows(token_rows, grad_qkv_rows).reshape(w_qkv.shape)
    input_grad = grad_one + scatter_rows(contract_cols(grad_qkv_rows, qkv_matrix))
    grad_vectors = jnp.stack(
        (
            grad_out_bias,
            grad_gain_one,
            grad_shift_one,
            grad_down_bias,
            grad_gain_two,
            grad_shift_two,
        ),
        axis=0,
    )
    gradients = (
        lax.psum_scatter(
            grad_qkv_weight.astype(jnp.bfloat16), "dp", scatter_dimension=0, tiled=True
        ).astype(jnp.float32),
        lax.psum_scatter(
            grad_out.astype(jnp.bfloat16), "dp", scatter_dimension=0, tiled=True
        ).astype(jnp.float32),
        lax.psum_scatter(
            grad_up.astype(jnp.bfloat16), "dp", scatter_dimension=1, tiled=True
        ).astype(jnp.float32),
        lax.psum_scatter(
            grad_down.astype(jnp.bfloat16), "dp", scatter_dimension=0, tiled=True
        ).astype(jnp.float32),
        lax.psum_scatter(
            grad_qkv_bias.astype(jnp.bfloat16), "dp", scatter_dimension=1, tiled=True
        ).astype(jnp.float32),
        lax.psum_scatter(
            grad_up_bias.astype(jnp.bfloat16), "dp", scatter_dimension=0, tiled=True
        ).astype(jnp.float32),
        lax.psum_scatter(
            grad_vectors.astype(jnp.bfloat16), "dp", scatter_dimension=1, tiled=True
        ).astype(jnp.float32),
    )
    correct_one = 1.0 - BETA_ONE**STEP
    correct_two = 1.0 - BETA_TWO**STEP
    results = []
    for master, first_old, second_old, gradient, step_rate, decay_rate in zip(
        masters, firsts, seconds, gradients, RATES, DECAYS
    ):
        new_first = BETA_ONE * first_old + (1.0 - BETA_ONE) * gradient
        new_second = BETA_TWO * second_old + (1.0 - BETA_TWO) * gradient * gradient
        direction = new_first / correct_one / (jnp.sqrt(new_second / correct_two) + EPS_ADAM)
        results.append(master - step_rate * (direction + decay_rate * master))
        results.append(new_first)
        results.append(new_second)
    return (block_out, input_grad) + tuple(results)


def solution(mesh):
    placed = (
        P("dp", ("col", "row")),
        P("dp"),
        P("dp", ("col", "row")),
        P(("col", "dp"), "row", None, None),
        P(("col", "dp"), "row", None, None),
        P(("col", "dp"), "row", None, None),
        P(("row", "dp"), "col"),
        P(("row", "dp"), "col"),
        P(("row", "dp"), "col"),
        P("col", ("row", "dp")),
        P("col", ("row", "dp")),
        P("col", ("row", "dp")),
        P(("row", "dp"), "col"),
        P(("row", "dp"), "col"),
        P(("row", "dp"), "col"),
        P(("row", "col"), "dp"),
        P(("row", "col"), "dp"),
        P(("row", "col"), "dp"),
        P(("row", "col", "dp")),
        P(("row", "col", "dp")),
        P(("row", "col", "dp")),
        P(None, ("col", "row", "dp")),
        P(None, ("col", "row", "dp")),
        P(None, ("col", "row", "dp")),
    )
    return jax.shard_map(
        shards,
        mesh=mesh,
        in_specs=placed,
        out_specs=(
            P("dp", ("col", "row")),
            P("dp", ("col", "row")),
            P(("col", "dp"), "row", None, None),
            P(("col", "dp"), "row", None, None),
            P(("col", "dp"), "row", None, None),
            P(("row", "dp"), "col"),
            P(("row", "dp"), "col"),
            P(("row", "dp"), "col"),
            P("col", ("row", "dp")),
            P("col", ("row", "dp")),
            P("col", ("row", "dp")),
            P(("row", "dp"), "col"),
            P(("row", "dp"), "col"),
            P(("row", "dp"), "col"),
            P(("row", "col"), "dp"),
            P(("row", "col"), "dp"),
            P(("row", "col"), "dp"),
            P(("row", "col", "dp")),
            P(("row", "col", "dp")),
            P(("row", "col", "dp")),
            P(None, ("col", "row", "dp")),
            P(None, ("col", "row", "dp")),
            P(None, ("col", "row", "dp")),
        ),
        check_vma=False,
    )
```

profile of v0, /device:TPU:0, one launch (start us, length us, event | category | flops | bytes accessed | tf_op | source)
XLA Modules:
  0.0 788.8 jit_solution(6695925796471425175)
XLA Ops:
  9.3 10.2 %all_gather.45 = bf16[1024,256]{1,0:T(8,128)(2,1)S(1)} all-gather(bf16[1024,128]{1,0:T(8,128)(2,1)} %param.24), channel_id=1, replica_groups=mesh['dp'=4,'row'=2,'col'=4] {'row'}, dimensions={1}, use_global_device_ids=true | all-gather | bytes 786432 | tf_op jit(solution)/shard_map/all_gather | solution.py:24
  19.5 29.3 %all_gather.46 = bf16[256,8,3,64]{3,1,2,0:T(8,128)(2,1)S(1)} all-gather(bf16[64,8,3,64]{3,1,2,0:T(8,128)(2,1)S(1)} %convert_element_type.132), channel_id=1, replica_groups=mesh['dp'=4,'row'=2,'col'=4] {'dp'}, dimensions={0}, use_global_device_ids=true | all-gather | bytes 983040 | tf_op jit(solution)/shard_map/all_gather | solution.py:127
  49.8 3.7 fusion.65
  54.2 11.3 %all-gather = bf16[4,48,2]{1,2,0:T(2,128)(2,1)S(1)} all-gather(bf16[1,48,2]{1,2,0:T(2,128)(2,1)S(1)} %convert_bitcast_fusion.7), channel_id=1, replica_groups=mesh['dp'=4,'row'=2,'col'=4] {'dp'}, dimensions={0}, use_global_device_ids=true | all-gather | bytes 960 | tf_op jit(solution)/shard_map/all_gather | solution.py:131
  66.0 47.5 %reduce-scatter.19.cloned.1.call-done = f32[1024,384]{1,0:T(8,128)} async-done(((f32[1024,1536]{1,0:T(8,128)}), f32[1024,384]{1,0:T(8,128)}) %reduce-scatter.19.cloned.1.call-update) | async-done | bytes 1572880 | tf_op jit(solution)/shard_map/reduce_scatter | solution.py:36
  121.5 14.1 %all_gather.49 = bf16[512,256]{1,0:T(8,128)(2,1)S(1)} all-gather(bf16[128,256]{1,0:T(8,128)(2,1)S(1)} %convert_element_type.139), channel_id=1, replica_groups=mesh['dp'=4,'row'=2,'col'=4] {'dp'}, dimensions={0}, use_global_device_ids=true | all-gather | bytes 327680 | tf_op jit(solution)/shard_map/all_gather | solution.py:128
  135.6 2.8 all-gather.10.cloned.1.call-done
  138.3 2.7 fusion.66
  141.9 11.9 %all-gather.1 = bf16[4,32,6]{1,2,0:T(8,128)(2,1)S(1)} all-gather(bf16[1,32,6]{1,2,0:T(8,128)(2,1)S(1)} %convert_bitcast_fusion), channel_id=1, replica_groups=mesh['dp'=4,'row'=2,'col'=4] {'dp'}, dimensions={0}, use_global_device_ids=true | all-gather | bytes 1920 | tf_op jit(solution)/shard_map/all_gather | solution.py:133
  154.0 7.6 reduce-scatter.21.cloned.1.call-done
  162.9 13.3 %all-reduce.4 = (f32[1024,1]{0,1:T(1,128)S(1)}, f32[1024,1]{0,1:T(1,128)S(1)}) all-reduce(f32[1024,1]{0,1:T(1,128)S(1)} %bitcast.174, f32[1024,1]{0,1:T(1,128)S(1)} %bitcast.173), channel_id=1, replica_groups=mesh['dp'=4,'row'=2,'col'=4] {'row','col'}, use_global_device_ids=true, to_apply=%region_7.8 | all-reduce | flops 2048 | bytes 16384 | tf_op jit(solution)/shard_map/psum | solution.py:40
  176.6 7.8 all_gather.51
  184.5 5.9 fusion.67
  192.3 10.4 %all-gather.2 = bf16[4,1,128]{2,1,0:T(2,128)(2,1)S(1)} all-gather(bf16[1,1,128]{2,1,0:T(2,128)(2,1)S(1)} %convert_bitcast_fusion.6), channel_id=1, replica_groups=mesh['dp'=4,'row'=2,'col'=4] {'dp'}, dimensions={0}, use_global_device_ids=true | all-gather | bytes 1280 | tf_op jit(solution)/shard_map/all_gather | solution.py:132
  202.7 59.0 %reduce-scatter.23.cloned.1.call-done = f32[1024,512]{1,0:T(8,128)} async-done(((f32[1024,2048]{1,0:T(8,128)}), f32[1024,512]{1,0:T(8,128)}) %reduce-scatter.23.cloned.1.call-update) | async-done | bytes 2097168 | tf_op jit(solution)/shard_map/reduce_scatter | solution.py:36
  261.7 6.7 multiply_convert_fusion.1
  268.7 34.2 %all-gather.14.cloned.1.call-done = bf16[1024,2048]{1,0:T(8,128)(2,1)} async-done(((bf16[1024,512]{1,0:T(8,128)(2,1)}), bf16[1024,2048]{1,0:T(8,128)(2,1)}) %all-gather.14.cloned.1.call-update) | async-done | bytes 4194320 | tf_op jit(solution)/shard_map/all_gather | solution.py:32
  302.9 4.7 fusion.68
  307.7 20.4 %reduce-scatter.25.cloned.1.call-done = f32[1024,128]{1,0:T(8,128)} async-done(((f32[1024,256]{1,0:T(8,128)}), f32[1024,128]{1,0:T(8,128)}) %reduce-scatter.25.cloned.1.call-update) | async-done | bytes 524304 | tf_op jit(solution)/shard_map/reduce_scatter | solution.py:28
  329.8 13.1 %all-reduce.3 = (f32[1024,1]{0,1:T(1,128)S(1)}, f32[1024,1]{0,1:T(1,128)S(1)}) all-reduce(f32[1024,1]{0,1:T(1,128)S(1)} %bitcast.172, f32[1024,1]{0,1:T(1,128)S(1)} %bitcast.171), channel_id=1, replica_groups=mesh['dp'=4,'row'=2,'col'=4] {'row','col'}, use_global_device_ids=true, to_apply=%region_13.14 | all-reduce | flops 2048 | bytes 16384 | tf_op jit(solution)/shard_map/psum | solution.py:40
  343.8 12.1 %all-reduce.2 = (f32[1024,1]{0,1:T(1,128)S(1)}, f32[1024,1]{0,1:T(1,128)S(1)}) all-reduce(f32[1024,1]{0,1:T(1,128)S(1)} %bitcast.175, f32[1024,1]{0,1:T(1,128)S(1)} %bitcast.176), channel_id=1, replica_groups=mesh['dp'=4,'row'=2,'col'=4] {'row','col'}, use_global_device_ids=true, to_apply=%region_17.18 | all-reduce | flops 2048 | bytes 16384 | tf_op jit(solution)/shard_map/psum | solution.py:40
  357.9 8.7 %all_gather.56 = bf16[1024,256]{1,0:T(8,128)(2,1)S(1)} all-gather(bf16[1024,128]{1,0:T(8,128)(2,1)S(1)} %convert_element_type.150), channel_id=1, replica_groups=mesh['dp'=4,'row'=2,'col'=4] {'row'}, dimensions={1}, use_global_device_ids=true | all-gather | bytes 786432 | tf_op jit(solution)/shard_map/all_gather | solution.py:24
  366.6 4.6 fusion.69
  371.3 71.6 %reduce-scatter.27.cloned.1.call-done = f32[1024,512]{1,0:T(8,128)} async-done(((f32[1024,2048]{1,0:T(8,128)}), f32[1024,512]{1,0:T(8,128)}) %reduce-scatter.27.cloned.1.call-update) | async-done | bytes 2097168 | tf_op jit(solution)/shard_map/reduce_scatter | solution.py:36
  442.9 4.8 fusion.51
  447.7 34.4 %all-gather.18.cloned.1.call-done = bf16[1024,2048]{1,0:T(8,128)(2,1)} async-done(((bf16[1024,512]{1,0:T(8,128)(2,1)}), bf16[1024,2048]{1,0:T(8,128)(2,1)}) %all-gather.18.cloned.1.call-update) | async-done | bytes 4194320 | tf_op jit(solution)/shard_map/all_gather | solution.py:32
  482.1 4.8 fusion.70
  487.0 20.4 %reduce-scatter.29.cloned.1.call-done = f32[1024,128]{1,0:T(8,128)} async-done(((f32[1024,256]{1,0:T(8,128)}), f32[1024,128]{1,0:T(8,128)}) %reduce-scatter.29.cloned.1.call-update) | async-done | bytes 524304 | tf_op jit(solution)/shard_map/reduce_scatter | solution.py:28
  509.6 13.1 %all-reduce.1 = (f32[1024,1]{0,1:T(1,128)S(1)}, f32[1024,1]{0,1:T(1,128)S(1)}) all-reduce(f32[1024,1]{0,1:T(1,128)S(1)} %bitcast.168, f32[1024,1]{0,1:T(1,128)S(1)} %bitcast.169), channel_id=1, replica_groups=mesh['dp'=4,'row'=2,'col'=4] {'row','col'}, use_global_device_ids=true, to_apply=%region_23.24 | all-reduce | flops 2048 | bytes 16384 | tf_op jit(solution)/shard_map/psum | solution.py:40
  523.9 7.8 all_gather.58
  533.9 30.6 %reduce-scatter.31.cloned.1.call-done = f32[1024,128]{1,0:T(8,128)} async-done(((f32[1024,512]{1,0:T(8,128)}), f32[1024,128]{1,0:T(8,128)}) %reduce-scatter.31.cloned.1.call-update) | async-done | bytes 524304 | tf_op jit(solution)/shard_map/reduce_scatter | solution.py:36
  566.2 3.1 fusion.12
  575.3 4.6 convolution_convert_fusion
  580.1 4.9 convolution_convert_fusion.1
  586.7 2.5 convolution_convert_fusion.3
  590.3 13.4 %all-gather.20.cloned.1.call-done = bf16[1024,1536]{0,1:T(8,128)(2,1)} async-done(((bf16[1024,384]{0,1:T(8,128)(2,1)}), bf16[1024,1536]{0,1:T(8,128)(2,1)}) %all-gather.20.cloned.1.call-update) | async-done | bytes 3145744 | tf_op jit(solution)/shard_map/all_gather | solution.py:32
  603.8 2.9 convolution_convert_fusion.2
  608.6 4.0 fusion.72
  613.9 19.3 %reduce-scatter.41.cloned.1.call-done = bf16[512,256]{1,0:T(8,128)(2,1)} async-done(((bf16[2048,256]{1,0:T(8,128)(2,1)}), bf16[512,256]{1,0:T(8,128)(2,1)}) %reduce-scatter.41.cloned.1.call-update) | async-done | bytes 262160 | tf_op jit(solution)/shard_map/reduce_scatter | solution.py:239
  635.5 9.3 %all-reduce = bf16[512]{0:T(512)(128)(2,1)S(1)} all-reduce(bf16[512]{0:T(512)(128)(2,1)S(1)} %copy-done.40), channel_id=15, replica_groups=mesh['dp'=4,'row'=2,'col'=4] {'dp'}, use_global_device_ids=true, to_apply=%region_34.35.clone | all-reduce | flops 512 | bytes 2048
  645.5 15.6 %reduce-scatter.39.cloned.1.call-done = bf16[256,512]{1,0:T(8,128)(2,1)} async-done(((bf16[256,2048]{1,0:T(8,128)(2,1)}), bf16[256,512]{1,0:T(8,128)(2,1)}) %reduce-scatter.39.cloned.1.call-update) | async-done | bytes 262160 | tf_op jit(solution)/shard_map/reduce_scatter | solution.py:236
  661.1 2.7 multiply_subtract_fusion.2
  663.8 17.7 %reduce-scatter.45.cloned.1.call-done = bf16[32,6]{1,0:T(8,128)(2,1)} async-done(((bf16[128,6]{1,0:T(8,128)(2,1)}), bf16[32,6]{1,0:T(8,128)(2,1)}) %reduce-scatter.45.cloned.1.call-update) | async-done | bytes 400
  682.9 19.2 %reduce-scatter.37.cloned.1.call-done = bf16[128,256]{1,0:T(8,128)(2,1)} async-done(((bf16[512,256]{1,0:T(8,128)(2,1)}), bf16[128,256]{1,0:T(8,128)(2,1)}) %reduce-scatter.37.cloned.1.call-update) | async-done | bytes 65552 | tf_op jit(solution)/shard_map/reduce_scatter | solution.py:233
  703.9 18.3 %reduce-scatter.43.cloned.1.call-done = bf16[48,2]{1,0:T(8,128)(2,1)} async-done(((bf16[192,2]{1,0:T(8,128)(2,1)}), bf16[48,2]{1,0:T(8,128)(2,1)}) %reduce-scatter.43.cloned.1.call-update) | async-done | bytes 208
  724.3 33.6 %reduce-scatter.35.cloned.1.call-done = bf16[64,8,3,64]{3,1,2,0:T(8,128)(2,1)} async-done(((bf16[256,8,3,64]{3,1,2,0:T(8,128)(2,1)}), bf16[64,8,3,64]{3,1,2,0:T(8,128)(2,1)}) %reduce-scatter.35.cloned.1.call-update) | async-done | bytes 196624 | tf_op jit(solution)/shard_map/reduce_scatter | solution.py:230
  757.9 2.8 multiply_subtract_fusion
  760.7 18.6 %reduce-scatter.33.cloned.1.call-done = f32[1024,128]{1,0:T(8,128)} async-done(((f32[1024,256]{1,0:T(8,128)}), f32[1024,128]{1,0:T(8,128)}) %reduce-scatter.33.cloned.1.call-update) | async-done | bytes 524304 | tf_op jit(solution)/shard_map/reduce_scatter | solution.py:28
  (219 shorter events, 49.6 us)
Async XLA Ops:
  8.0 105.5 %reduce-scatter.19.cloned.1.call-start = ((), (), s32[]{:S(2)}) async-start(), calls=%async_computation.14 | async-start | bytes 7864320 | tf_op jit(solution)/shard_map/reduce_scatter | solution.py:36
  19.4 30.4 %copy-start.3 = (bf16[1024,256]{1,0:T(8,128)(2,1)}, bf16[1024,256]{1,0:T(8,128)(2,1)S(1)}, u32[]{:S(2)}) copy-start(bf16[1024,256]{1,0:T(8,128)(2,1)S(1)} %all_gather.45) | copy-start | bytes 1572868
  53.5 12.2 %copy-start.41 = (s32[1024]{0:T(1024)S(1)}, s32[1024]{0:T(1024)}, u32[]{:S(2)}) copy-start(s32[1024]{0:T(1024)} %param.25) | copy-start | bytes 12292
  53.5 84.8 %all-gather.10.cloned.1.call-start = ((), (), s32[]{:S(2)}) async-start(), calls=%async_computation.15 | async-start | bytes 1310720 | tf_op jit(solution)/shard_map/all_gather | solution.py:32
  121.4 19.7 %copy-start.17 = (f32[256,512]{1,0:T(8,128)S(1)}, f32[256,512]{1,0:T(8,128)}, u32[]{:S(2)}) copy-start(f32[256,512]{1,0:T(8,128)} %param.33) | copy-start | bytes 1572868
  121.4 40.1 %reduce-scatter.21.cloned.1.call-start = ((), (), s32[]{:S(2)}) async-start(), calls=%async_computation.16 | async-start | bytes 1572864 | tf_op jit(solution)/shard_map/reduce_scatter | solution.py:28
  135.6 6.4 copy-start.36
  135.6 26.0 %copy-start.21 = (bf16[1024,128]{1,0:T(8,128)(2,1)S(1)}, bf16[1024,128]{1,0:T(8,128)(2,1)}, u32[]{:S(2)}) copy-start(bf16[1024,128]{1,0:T(8,128)(2,1)} %param.24) | copy-start | bytes 786436
  141.0 43.4 %all-gather.12.cloned.1.call-start = ((), (), s32[]{:S(2)}) async-start(), calls=%async_computation.17 | async-start | bytes 1310720 | tf_op jit(solution)/shard_map/all_gather | solution.py:129
  141.9 119.8 %reduce-scatter.23.cloned.1.call-start = ((), (), s32[]{:S(2)}) async-start(), calls=%async_computation.18 | async-start | bytes 10485760 | tf_op jit(solution)/shard_map/reduce_scatter | solution.py:36
  154.0 174.1 %copy-start.38 = (f32[128]{0:T(128)}, f32[128]{0:T(128)S(1)}, u32[]{:S(2)}) copy-start(f32[128]{0:T(128)S(1)} %get-tuple-element.84) | copy-start | bytes 1540
  190.5 78.3 %all-gather.16.cloned.1.call-start = ((), (), s32[]{:S(2)}) async-start(), calls=%async_computation.20 | async-start | bytes 1310720 | tf_op jit(solution)/shard_map/all_gather | solution.py:130
  192.2 110.7 %all-gather.14.cloned.1.call-start = ((), (), s32[]{:S(2)}) async-start(), calls=%async_computation.19 | async-start | bytes 5242880 | tf_op jit(solution)/shard_map/all_gather | solution.py:32
  202.7 65.7 %copy-start.35 = (f32[4,1,128]{2,1,0:T(1,128)}, f32[4,1,128]{2,1,0:T(1,128)S(1)}, u32[]{:S(2)}) copy-start(f32[4,1,128]{2,1,0:T(1,128)S(1)} %convert_element_type.175) | copy-start | bytes 6148
  268.4 59.6 %reduce-scatter.25.cloned.1.call-start = ((), (), s32[]{:S(2)}) async-start(), calls=%async_computation.21 | async-start | bytes 1572864 | tf_op jit(solution)/shard_map/reduce_scatter | solution.py:28
  307.6 35.4 %copy-start.12 = (bf16[1024,128]{1,0:T(8,128)(2,1)S(1)}, bf16[1024,128]{1,0:T(8,128)(2,1)}, u32[]{:S(2)}) copy-start(bf16[1024,128]{1,0:T(8,128)(2,1)} %param.26) | copy-start | bytes 786436
  307.6 135.2 %reduce-scatter.27.cloned.1.call-start = ((), (), s32[]{:S(2)}) async-start(), calls=%async_computation.22 | async-start | bytes 10485760 | tf_op jit(solution)/shard_map/reduce_scatter | solution.py:36
  329.8 36.8 %copy-start.20 = (bf16[2048,256]{1,0:T(8,128)(2,1)S(1)}, bf16[2048,256]{1,0:T(8,128)(2,1)}, u32[]{:S(2)}) copy-start(bf16[2048,256]{1,0:T(8,128)(2,1)} %all-gather.16.cloned.1.call-done) | copy-start | bytes 3145732
  371.2 71.7 %copy-start.2 = (f32[1024,512]{1,0:T(8,128)S(1)}, f32[1024,512]{1,0:T(8,128)}, u32[]{:S(2)}) copy-start(f32[1024,512]{1,0:T(8,128)} %reduce-scatter.23.cloned.1.call-done) | copy-start | bytes 6291460
  371.2 110.9 %all-gather.18.cloned.1.call-start = ((), (), s32[]{:S(2)}) async-start(), calls=%async_computation.23 | async-start | bytes 5242880 | tf_op jit(solution)/shard_map/all_gather | solution.py:32
  447.7 59.7 %copy-start.39 = (f32[128]{0:T(128)S(1)}, f32[128]{0:T(128)}, u32[]{:S(2)}) copy-start(f32[128]{0:T(128)} %copy-done.38) | copy-start | bytes 1540
  447.7 59.7 %reduce-scatter.29.cloned.1.call-start = ((), (), s32[]{:S(2)}) async-start(), calls=%async_computation.24 | async-start | bytes 1572864 | tf_op jit(solution)/shard_map/reduce_scatter | solution.py:28
  486.9 77.6 %reduce-scatter.31.cloned.1.call-start = ((), (), s32[]{:S(2)}) async-start(), calls=%async_computation.25 | async-start | bytes 2621440 | tf_op jit(solution)/shard_map/reduce_scatter | solution.py:36
  509.6 22.1 %copy-start.14 = (bf16[512,256]{1,0:T(8,128)(2,1)S(1)}, bf16[512,256]{1,0:T(8,128)(2,1)}, u32[]{:S(2)}) copy-start(bf16[512,256]{1,0:T(8,128)(2,1)} %copy-done.13) | copy-start | bytes 786436
  533.6 70.2 %all-gather.20.cloned.1.call-start = ((), (), s32[]{:S(2)}) async-start(), calls=%async_computation.26 | async-start | bytes 3932160 | tf_op jit(solution)/shard_map/all_gather | solution.py:32
  575.3 57.9 %reduce-scatter.41.cloned.1.call-start = ((), (), s32[]{:S(2)}) async-start(), calls=%async_computation.31 | async-start | bytes 1310720 | tf_op jit(solution)/shard_map/reduce_scatter | solution.py:239
  580.0 81.1 %reduce-scatter.39.cloned.1.call-start = ((), (), s32[]{:S(2)}) async-start(), calls=%async_computation.30 | async-start | bytes 1310720 | tf_op jit(solution)/shard_map/reduce_scatter | solution.py:236
  585.0 18.8 %copy-start.4 = (bf16[1024,256]{1,0:T(8,128)(2,1)S(1)}, bf16[1024,256]{1,0:T(8,128)(2,1)}, u32[]{:S(2)}) copy-start(bf16[1024,256]{1,0:T(8,128)(2,1)} %copy-done.3) | copy-start | bytes 1572868
  585.0 96.5 %reduce-scatter.45.cloned.1.call-start = ((), (), s32[]{:S(2)}) async-start(), calls=%async_computation.33 | async-start | bytes 40960
  586.7 115.4 %reduce-scatter.37.cloned.1.call-start = ((), (), s32[]{:S(2)}) async-start(), calls=%async_computation.29 | async-start | bytes 327680 | tf_op jit(solution)/shard_map/reduce_scatter | solution.py:233
  589.3 133.0 %reduce-scatter.43.cloned.1.call-start = ((), (), s32[]{:S(2)}) async-start(), calls=%async_computation.32 | async-start | bytes 61440
  590.3 167.6 %reduce-scatter.35.cloned.1.call-start = ((), (), s32[]{:S(2)}) async-start(), calls=%async_computation.28 | async-start | bytes 1966080 | tf_op jit(solution)/shard_map/reduce_scatter | solution.py:230
  608.5 24.7 %copy-start.16 = (f32[512,256]{1,0:T(8,128)S(1)}, f32[512,256]{1,0:T(8,128)}, u32[]{:S(2)}) copy-start(f32[512,256]{1,0:T(8,128)} %param.36) | copy-start | bytes 1572868
  608.5 24.7 %copy-start.31 = (f32[512,256]{1,0:T(8,128)S(1)}, f32[512,256]{1,0:T(8,128)}, u32[]{:S(2)}) copy-start(f32[512,256]{1,0:T(8,128)} %param.37) | copy-start | bytes 1572868
  608.5 24.7 %copy-start.32 = (f32[512,256]{1,0:T(8,128)S(1)}, f32[512,256]{1,0:T(8,128)}, u32[]{:S(2)}) copy-start(f32[512,256]{1,0:T(8,128)} %param.38) | copy-start | bytes 1572868
  608.5 170.7 %reduce-scatter.33.cloned.1.call-start = ((), (), s32[]{:S(2)}) async-start(), calls=%async_computation.27 | async-start | bytes 1572864 | tf_op jit(solution)/shard_map/reduce_scatter | solution.py:28
  612.6 22.9 %copy-start.40 = (bf16[512]{0:T(512)(128)(2,1)S(1)}, bf16[512]{0:T(512)(128)(2,1)}, u32[]{:S(2)}) copy-start(bf16[512]{0:T(512)(128)(2,1)} %get-tuple-element.52) | copy-start | bytes 3076
  612.6 32.3 %copy-start.51 = (f32[128]{0:T(128)S(1)}, f32[128]{0:T(128)}, u32[]{:S(2)}) copy-start(f32[128]{0:T(128)} %param.42) | copy-start | bytes 1540
  612.6 32.3 %copy-start.52 = (f32[128]{0:T(128)S(1)}, f32[128]{0:T(128)}, u32[]{:S(2)}) copy-start(f32[128]{0:T(128)} %param.43) | copy-start | bytes 1540
  612.6 32.3 %copy-start.53 = (f32[128]{0:T(128)S(1)}, f32[128]{0:T(128)}, u32[]{:S(2)}) copy-start(f32[128]{0:T(128)} %param.44) | copy-start | bytes 1540
  612.6 48.5 %copy-start.18 = (f32[256,512]{1,0:T(8,128)S(1)}, f32[256,512]{1,0:T(8,128)}, u32[]{:S(2)}) copy-start(f32[256,512]{1,0:T(8,128)} %param.33) | copy-start | bytes 1572868
  635.5 46.8 %copy-start.37 = (f32[6,32]{1,0:T(8,128)S(1)}, f32[6,32]{1,0:T(8,128)}, u32[]{:S(2)}) copy-start(f32[6,32]{1,0:T(8,128)} %param.45) | copy-start | bytes 2308
  635.5 46.8 %copy-start.42 = (f32[6,32]{1,0:T(8,128)S(1)}, f32[6,32]{1,0:T(8,128)}, u32[]{:S(2)}) copy-start(f32[6,32]{1,0:T(8,128)} %param.46) | copy-start | bytes 2308
  635.5 46.8 %copy-start.43 = (f32[6,32]{1,0:T(8,128)S(1)}, f32[6,32]{1,0:T(8,128)}, u32[]{:S(2)}) copy-start(f32[6,32]{1,0:T(8,128)} %param.47) | copy-start | bytes 2308
  645.5 77.5 %copy-start.49 = (f32[2,48]{1,0:T(2,128)S(1)}, f32[2,48]{1,0:T(2,128)}, u32[]{:S(2)}) copy-start(f32[2,48]{1,0:T(2,128)} %param.39) | copy-start | bytes 1156
  645.5 112.4 %copy-start.5 = (f32[64,8,3,64]{3,1,2,0:T(8,128)S(1)}, f32[64,8,3,64]{3,1,2,0:T(8,128)}, u32[]{:S(2)}) copy-start(f32[64,8,3,64]{3,1,2,0:T(8,128)} %param.27) | copy-start | bytes 1179652
  645.5 112.4 %copy-start.28 = (f32[64,8,3,64]{3,1,2,0:T(8,128)S(1)}, f32[64,8,3,64]{3,1,2,0:T(8,128)}, u32[]{:S(2)}) copy-start(f32[64,8,3,64]{3,1,2,0:T(8,128)} %param.28) | copy-start | bytes 1179652
  645.5 112.4 %copy-start.29 = (f32[64,8,3,64]{3,1,2,0:T(8,128)S(1)}, f32[64,8,3,64]{3,1,2,0:T(8,128)}, u32[]{:S(2)}) copy-start(f32[64,8,3,64]{3,1,2,0:T(8,128)} %param.29) | copy-start | bytes 1179652
  (27 other events, 80.8 us)
Sparse Core Ops, SparseCore 0:
  53.6 59.8 reduce-scatter.18
  121.5 16.7 all-gather.9
  141.2 20.3 reduce-scatter.20
  190.6 71.0 reduce-scatter.22
  307.7 20.3 reduce-scatter.24
  487.0 20.3 reduce-scatter.28
Sparse Core Ops, SparseCore 1:
  143.7 27.8 all-gather.11
  193.2 27.2 all-gather.15
  268.5 34.3 all-gather.13
  371.3 71.5 reduce-scatter.26
  447.8 34.3 all-gather.17
  533.6 30.8 reduce-scatter.30
  575.3 28.4 all-gather.19
  606.0 27.1 reduce-scatter.40
  635.4 25.7 reduce-scatter.38
  664.1 17.4 reduce-scatter.44
  684.2 17.8 reduce-scatter.36
  705.0 17.1 reduce-scatter.42
  724.4 33.4 reduce-scatter.34
  760.2 19.0 reduce-scatter.32
where the time goes:
time: 790 us; the launch traced here: 789 us
  waiting for transfers between devices  484 us (61%)
  blocking collectives  173 us (22%)
  matrix products  54.1 us (7%)
  other arithmetic  43.1 us (5%)
  between operations  17.3 us (2%)
  local copies, waits for them, and re-layouts  16 us (2%)
    reduce_scatter x4, waiting for transfers between devices, scatter_cols(): lax.psum_scatter(partial_terms, 'col', scatter_dimension=1, tiled=True)  209 us
    all_gather x4, waiting for transfers between devices, gather_cols(): return lax.all_gather(shard_block, 'col', axis=1, tiled=True)  84.7 us
    reduce_scatter x4, waiting for transfers between devices, scatter_rows(): lax.psum_scatter(partial_terms, 'row', scatter_dimension=1, tiled=True)  67 us
    psum x4, blocking collectives, feature_sums(): return lax.psum((first_term, second_term), ('row', 'col'))  51.7 us
    unnamed x22, waiting for transfers between devices  36.3 us
    all_gather x4, blocking collectives, gather_rows(): return lax.all_gather(shard_block, 'row', axis=1, tiled=True)  34.5 us
    reduce_scatter x1, waiting for transfers between devices, shards(): lax.psum_scatter(grad_qkv_weight.astype(jnp.bfloat16), 'dp', scatter_dime...  33.6 us
    all_gather x1, blocking collectives, shards(): lax.all_gather(qkv_weight.astype(bf16), 'dp', axis=0, tiled=True)  29.3 us
  transfers between devices with their start and end apart: 20, of which 18 were waited for; matrix products, arithmetic and copies ran while one was open for 6% of the time, Pallas kernels for 0%

commit v1 on v0

--- a/solution.py
+++ b/solution.py
@@ -20,24 +20,35 @@
 DECAYS = (0.01, 0.01, 0.01, 0.01, 0.0, 0.0, 0.0)
 
 
-def gather_rows(shard_block):
-    return lax.all_gather(shard_block, "row", axis=1, tiled=True)
-
-
-def scatter_rows(partial_terms):
-    return lax.psum_scatter(partial_terms, "row", scatter_dimension=1, tiled=True)
-
-
-def gather_cols(shard_block):
-    return lax.all_gather(shard_block, "col", axis=1, tiled=True)
-
-
-def scatter_cols(partial_terms):
-    return lax.psum_scatter(partial_terms, "col", scatter_dimension=1, tiled=True)
-
-
-def feature_sums(first_term, second_term):
-    return lax.psum((first_term, second_term), ("row", "col"))
+GROUP = ("col", "row")
+
+
+def group_gather(block):
+    return lax.all_gather(block, GROUP, axis=0, tiled=True)
+
+
+def feature_gather(block):
+    return lax.all_gather(block, GROUP, axis=1, tiled=True)
+
+
+def group_scatter(partial_terms):
+    return lax.psum_scatter(
+        partial_terms.astype(jnp.bfloat16), GROUP, scatter_dimension=0, tiled=True
+    ).astype(jnp.float32)
+
+
+def feature_scatter(partial_terms):
+    return lax.psum_scatter(
+        partial_terms.astype(jnp.bfloat16), GROUP, scatter_dimension=1, tiled=True
+    ).astype(jnp.float32)
+
+
+def to_tokens(block):
+    return lax.all_to_all(block, GROUP, split_axis=0, concat_axis=1, tiled=True)
+
+
+def to_features(block):
+    return lax.all_to_all(block, GROUP, split_axis=1, concat_axis=0, tiled=True)
 
 
 def contract_rows(left_side, right_side):
@@ -57,22 +68,17 @@
 
 
 def norm_forward(residual, norm_gain, norm_shift):
-    sum_first, sum_second = feature_sums(
-        jnp.sum(residual, axis=1, keepdims=True),
-        jnp.sum(residual * residual, axis=1, keepdims=True),
-    )
-    mean_row = sum_first / D
-    scale_row = lax.rsqrt(sum_second / D - mean_row * mean_row + EPS_NORM)
+    mean_row = jnp.sum(residual, axis=1, keepdims=True) / D
+    square_row = jnp.sum(residual * residual, axis=1, keepdims=True) / D
+    scale_row = lax.rsqrt(square_row - mean_row * mean_row + EPS_NORM)
     normed = (residual - mean_row) * scale_row
     return (normed * norm_gain + norm_shift, normed, scale_row)
 
 
 def norm_backward(grad_out, norm_gain, normed, scale_row):
     grad_normed = grad_out * norm_gain
-    sum_plain, sum_cross = feature_sums(
-        jnp.sum(grad_normed, axis=1, keepdims=True),
-        jnp.sum(grad_normed * normed, axis=1, keepdims=True),
-    )
+    sum_plain = jnp.sum(grad_normed, axis=1, keepdims=True)
+    sum_cross = jnp.sum(grad_normed * normed, axis=1, keepdims=True)
     grad_resid = scale_row * (grad_normed - sum_plain / D - normed * (sum_cross / D))
     return (grad_resid, jnp.sum(grad_out * normed, axis=0), jnp.sum(grad_out, axis=0))
 
@@ -123,27 +129,75 @@
     )
     bf16 = jnp.bfloat16
     f32 = jnp.float32
-    w_qkv, w_out, w_up, w_down, b_qkv, b_up, vectors = (
-        lax.all_gather(qkv_weight.astype(bf16), "dp", axis=0, tiled=True),
-        lax.all_gather(out_weight.astype(bf16), "dp", axis=0, tiled=True),
-        lax.all_gather(up_weight.astype(bf16), "dp", axis=1, tiled=True),
-        lax.all_gather(down_weight.astype(bf16), "dp", axis=0, tiled=True),
-        lax.all_gather(qkv_bias.astype(bf16), "dp", axis=1, tiled=True),
-        lax.all_gather(up_bias.astype(bf16), "dp", axis=0, tiled=True),
-        lax.all_gather(norm_vectors.astype(bf16), "dp", axis=1, tiled=True),
-    )
-    vector_rows = vectors.astype(f32)
+    n_dp, n_row, n_col = (lax.axis_size(name) for name in ("dp", "row", "col"))
+    at_dp, at_row, at_col = (lax.axis_index(name) for name in ("dp", "row", "col"))
+    at_group = at_col * n_row + at_row
     tok_count = tokens.shape[0]
+    own_tok = tok_count // (n_row * n_col)
     seq_count = tok_count // SEQ
-    heads_local = b_qkv.shape[0]
     score_scale = 1.0 / math.sqrt(HD)
-    qkv_matrix = w_qkv.reshape(w_qkv.shape[0], -1)
+    qkv_rows, heads_row = qkv_weight.shape[:2]
+    heads_local = heads_row // n_col
+    width = heads_local * 3 * HD
+    feats = heads_local * HD
+    d_col = D // n_col
+    ff_own = up_weight.shape[1] // n_col
+    ff_local = ff_own * n_dp
+    w_qkv = lax.all_gather(
+        lax.all_to_all(
+            qkv_weight.astype(bf16).reshape(qkv_rows, n_col, width), "col", 1, 0, tiled=True
+        ).reshape(n_col, qkv_rows, width),
+        "dp",
+        axis=1,
+    ).reshape(D, width)
+    w_out = (
+        lax.all_to_all(
+            lax.all_gather(out_weight.astype(bf16), "dp", axis=0, tiled=True).reshape(
+                n_col, feats, d_col
+            ),
+            "col",
+            0,
+            2,
+            tiled=True,
+        )
+    ).reshape(feats, D)
+    w_up = lax.all_gather(
+        lax.all_to_all(up_weight.astype(bf16).T, "col", 0, 1, tiled=True), "dp", axis=0, tiled=True
+    )
+    w_down = lax.all_gather(
+        lax.all_to_all(down_weight.astype(bf16), "col", 0, 1, tiled=True), "dp", axis=0, tiled=True
+    )
+    n_vec = norm_vectors.shape[1]
+    small = lax.all_gather(
+        jnp.concatenate(
+            (norm_vectors.reshape(-1), qkv_bias.reshape(-1), up_bias.reshape(-1))
+        ).astype(bf16),
+        ("col", "row", "dp"),
+        axis=0,
+    ).astype(f32)
+    vec_size, qb_size = norm_vectors.size, qkv_bias.size
+    vector_rows = (
+        small[:, :vec_size].reshape(-1, 6, n_vec).transpose(1, 0, 2).reshape(6, D)
+    )
+    small_group = small.reshape(n_col, n_row, n_dp, -1)
+    qb_all = lax.dynamic_index_in_dim(
+        small_group[..., vec_size : vec_size + qb_size].reshape(n_col * n_row, n_dp, -1),
+        at_group,
+        0,
+        keepdims=False,
+    )
+    b_qkv = qb_all.reshape(n_dp, heads_local, -1).transpose(1, 0, 2).reshape(-1)
+    ub_all = lax.dynamic_index_in_dim(
+        small_group[..., vec_size + qb_size :], at_row, 1, keepdims=False
+    ).reshape(n_dp, n_col, ff_own)
+    b_up = lax.dynamic_index_in_dim(ub_all, at_col, 1, keepdims=False).reshape(-1)
+
     seg_rows = segment_ids.reshape(seq_count, SEQ)
     same_doc = seg_rows[:, None, :, None] == seg_rows[:, None, None, :]
-    token_rows = gather_rows(tokens)
-    qkv_local = scatter_cols(
-        jnp.dot(token_rows, qkv_matrix, preferred_element_type=f32)
-    ) + b_qkv.astype(f32).reshape(-1)
+    token_rows = feature_gather(tokens)
+    own_tokens = lax.dynamic_slice_in_dim(token_rows, at_group * own_tok, own_tok, 0)
+    own_out_grad = to_tokens(out_grad).astype(f32)
+    qkv_local = jnp.dot(token_rows, w_qkv, preferred_element_type=f32) + b_qkv
     qkv_low = qkv_local.astype(bf16).reshape(seq_count, SEQ, heads_local, 3, HD)
     queries = qkv_low[:, :, :, 0]
     key_rows = qkv_low[:, :, :, 1]
@@ -154,47 +208,56 @@
     row_total = jnp.sum(exp_scores, axis=-1, keepdims=True)
     log_total = row_peak + jnp.log(row_total)
     soft_low = (exp_scores / row_total).astype(bf16)
-    attended = jnp.einsum("shqk,skhd->sqhd", soft_low, value_rows, preferred_element_type=f32)
-    attended_rows = gather_cols(attended.reshape(tok_count, heads_local * HD).astype(bf16))
+    attended = (
+        jnp.einsum("shqk,skhd->sqhd", soft_low, value_rows, preferred_element_type=f32)
+        .reshape(tok_count, feats)
+        .astype(bf16)
+    )
     residual_one = (
-        tokens.astype(f32)
-        + scatter_rows(jnp.dot(attended_rows, w_out, preferred_element_type=f32))
+        own_tokens.astype(f32)
+        + group_scatter(jnp.dot(attended, w_out, preferred_element_type=f32))
         + vector_rows[0]
     )
     hidden_one, normed_one, scale_one = norm_forward(residual_one, vector_rows[1], vector_rows[2])
-    hidden_rows = gather_rows(hidden_one.astype(bf16))
-    pre_act = scatter_cols(jnp.dot(hidden_rows, w_up, preferred_element_type=f32)) + b_up.astype(
-        f32
-    )
-    act_rows = gather_cols(gelu_exact(pre_act).astype(bf16))
+    hidden_rows = group_gather(hidden_one.astype(bf16))
+    pre_act = contract_cols(hidden_rows, w_up) + b_up
+    act_rows = gelu_exact(pre_act).astype(bf16)
     residual_two = (
         hidden_one
-        + scatter_rows(jnp.dot(act_rows, w_down, preferred_element_type=f32))
+        + group_scatter(jnp.dot(act_rows, w_down, preferred_element_type=f32))
         + vector_rows[3]
     )
     output_rows, normed_two, scale_two = norm_forward(residual_two, vector_rows[4], vector_rows[5])
-    block_out = output_rows.astype(bf16)
+    block_out = to_features(output_rows.astype(bf16))
     grad_two, grad_gain_two, grad_shift_two = norm_backward(
-        out_grad.astype(f32), vector_rows[4], normed_two, scale_two
+        own_out_grad, vector_rows[4], normed_two, scale_two
     )
     grad_down_bias = jnp.sum(grad_two, axis=0)
-    grad_two_rows = gather_rows(grad_two.astype(bf16))
-    grad_down = contract_rows(act_rows, grad_two_rows)
-    grad_act = scatter_cols(contract_cols(grad_two_rows, w_down))
+    grad_two_rows = group_gather(grad_two.astype(bf16))
+    grad_act = contract_cols(grad_two_rows, w_down)
     gelu_value, gelu_pull = jax.vjp(gelu_exact, pre_act)
     grad_pre = gelu_pull(grad_act)[0]
     grad_up_bias = jnp.sum(grad_pre, axis=0)
-    grad_pre_rows = gather_cols(grad_pre.astype(bf16))
-    grad_up = contract_rows(hidden_rows, grad_pre_rows)
-    grad_hidden = grad_two + scatter_rows(contract_cols(grad_pre_rows, w_up))
+    grad_pre_low = grad_pre.astype(bf16)
+    grad_hidden = grad_two + group_scatter(
+        jnp.dot(grad_pre_low, w_up, preferred_element_type=f32)
+    )
+    grad_down = lax.psum_scatter(
+        contract_rows(act_rows, grad_two_rows).astype(bf16), "dp", scatter_dimension=0, tiled=True
+    )
+    grad_up = lax.psum_scatter(
+        contract_rows(grad_pre_low, hidden_rows).astype(bf16),
+        "dp",
+        scatter_dimension=0,
+        tiled=True,
+    )
     grad_one, grad_gain_one, grad_shift_one = norm_backward(
         grad_hidden, vector_rows[1], normed_one, scale_one
     )
     grad_out_bias = jnp.sum(grad_one, axis=0)
-    grad_one_rows = gather_rows(grad_one.astype(bf16))
-    grad_out = contract_rows(attended_rows, grad_one_rows)
-    grad_att = scatter_cols(contract_cols(grad_one_rows, w_out))
-    grad_att_low = grad_att.astype(bf16).reshape(seq_count, SEQ, heads_local, HD)
+    grad_one_rows = group_gather(grad_one.astype(bf16))
+    grad_att_low = contract_cols(grad_one_rows, w_out).astype(bf16)
+    grad_att_low = grad_att_low.reshape(seq_count, SEQ, heads_local, HD)
     soft_again = jnp.exp(scores - log_total)
     grad_soft = jnp.einsum("sqhd,skhd->shqk", grad_att_low, value_rows, preferred_element_type=f32)
     grad_values = jnp.einsum(
@@ -211,10 +274,29 @@
         * score_scale
     )
     grad_qkv = jnp.stack((grad_queries, grad_keys, grad_values), axis=3).reshape(tok_count, -1)
-    grad_qkv_bias = jnp.sum(grad_qkv, axis=0).reshape(b_qkv.shape)
-    grad_qkv_rows = gather_cols(grad_qkv.astype(bf16))
-    grad_qkv_weight = contract_rows(token_rows, grad_qkv_rows).reshape(w_qkv.shape)
-    input_grad = grad_one + scatter_rows(contract_cols(grad_qkv_rows, qkv_matrix))
+    grad_qkv_bias = jnp.sum(grad_qkv, axis=0)
+    grad_qkv_low = grad_qkv.astype(bf16)
+    grad_qkv_weight = lax.psum_scatter(
+        contract_rows(token_rows, grad_qkv_low)
+        .astype(bf16)
+        .reshape(n_col, n_dp, qkv_rows, width)
+        .transpose(1, 0, 2, 3)
+        .reshape(D, width),
+        "dp",
+        scatter_dimension=0,
+        tiled=True,
+    ).reshape(n_col, qkv_rows, width)
+    input_grad = lax.dynamic_slice_in_dim(
+        grad_one_rows, at_group * tokens.shape[1], tokens.shape[1], 1
+    ).astype(f32) + feature_scatter(contract_cols(grad_qkv_low, w_qkv))
+    grad_out = lax.psum_scatter(
+        lax.all_to_all(
+            contract_rows(attended, grad_one_rows).astype(bf16), "col", 1, 0, tiled=True
+        ),
+        "dp",
+        scatter_dimension=0,
+        tiled=True,
+    )
     grad_vectors = jnp.stack(
         (
             grad_out_bias,
@@ -226,28 +308,37 @@
         ),
         axis=0,
     )
+    ub_place = lax.dynamic_update_slice(
+        jnp.zeros((n_row, n_dp, n_col, ff_own), f32),
+        grad_up_bias.reshape(1, n_dp, 1, ff_own),
+        (at_row, 0, at_col, 0),
+    )
+    sums = lax.psum(jnp.concatenate((grad_vectors.reshape(-1), ub_place.reshape(-1))), ("col", "row", "dp"))
+    grad_vectors = lax.dynamic_slice_in_dim(
+        sums[: 6 * D].reshape(6, D), (at_group * n_dp + at_dp) * n_vec, n_vec, 1
+    )
+    grad_up_bias = lax.dynamic_slice_in_dim(
+        sums[6 * D :],
+        ((at_row * n_col + at_col) * n_dp + at_dp) * up_bias.shape[0],
+        up_bias.shape[0],
+        0,
+    )
+    grad_qkv_bias = lax.dynamic_slice_in_dim(
+        lax.psum(grad_qkv_bias, "dp").reshape(heads_local, -1),
+        at_dp * qkv_bias.shape[1],
+        qkv_bias.shape[1],
+        1,
+    )
     gradients = (
-        lax.psum_scatter(
-            grad_qkv_weight.astype(jnp.bfloat16), "dp", scatter_dimension=0, tiled=True
-        ).astype(jnp.float32),
-        lax.psum_scatter(
-            grad_out.astype(jnp.bfloat16), "dp", scatter_dimension=0, tiled=True
-        ).astype(jnp.float32),
-        lax.psum_scatter(
-            grad_up.astype(jnp.bfloat16), "dp", scatter_dimension=1, tiled=True
-        ).astype(jnp.float32),
-        lax.psum_scatter(
-            grad_down.astype(jnp.bfloat16), "dp", scatter_dimension=0, tiled=True
-        ).astype(jnp.float32),
-        lax.psum_scatter(
-            grad_qkv_bias.astype(jnp.bfloat16), "dp", scatter_dimension=1, tiled=True
-        ).astype(jnp.float32),
-        lax.psum_scatter(
-            grad_up_bias.astype(jnp.bfloat16), "dp", scatter_dimension=0, tiled=True
-        ).astype(jnp.float32),
-        lax.psum_scatter(
-            grad_vectors.astype(jnp.bfloat16), "dp", scatter_dimension=1, tiled=True
-        ).astype(jnp.float32),
+        lax.all_to_all(grad_qkv_weight, "col", 0, 2, tiled=True)
+        .reshape(qkv_weight.shape)
+        .astype(f32),
+        grad_out.astype(f32),
+        lax.all_to_all(grad_up, "col", 1, 0, tiled=True).T.astype(f32),
+        lax.all_to_all(grad_down, "col", 1, 0, tiled=True).astype(f32),
+        grad_qkv_bias,
+        grad_up_bias,
+        grad_vectors,
     )
     correct_one = 1.0 - BETA_ONE**STEP
     correct_two = 1.0 - BETA_TWO**STEP

time: 790 us -> 556 us (0.70)
  waiting for transfers between devices: 484 us -> 215 us
  starting transfers between devices: 1.26 us -> 30 us
  local copies, waits for them, and re-layouts: 16 us -> 44 us
  other arithmetic: 43.1 us -> 28.4 us
    reduce_scatter x12 -> x7, waiting for transfers between devices: 363 us -> 106 us  [the longest x3 101 us: group_scatter(): lax.psum_scatter(partial_terms.astype(jnp.bfloat16), GROUP, scatter_dimen...]
    unnamed x22 -> x15, waiting for transfers between devices: 36.3 us -> 0.9 us
    all_to_all x0 -> x8, starting transfers between devices: none -> 29 us  [the longest x1 4.24 us: shards(): lax.all_to_all(qkv_weight.astype(bf16).reshape(qkv_rows, n_col, width), '...]
    all_to_all x0 -> x8, waiting for transfers between devices: none -> 20.1 us  [the longest x1 6.04 us: to_tokens(): return lax.all_to_all(block, GROUP, split_axis=0, concat_axis=1, tiled=True)]
    all_to_all x0 -> x2, blocking collectives: none -> 17.9 us  [the longest x1 9.09 us: shards(): lax.all_to_all(contract_rows(attended, grad_one_rows).astype(bf16), 'col'...]
    unnamed x117 -> x93, local copies, waits for them, and re-layouts: 9.08 us -> 25.1 us
    unnamed x1 -> x0, blocking collectives: 9.3 us -> none
    all_gather x8 -> x2, blocking collectives: 97.5 us -> 88.3 us  [the longest x1 70.4 us: shards(): lax.all_gather(jnp.concatenate((norm_vectors.reshape(-1), qkv_bias.reshap...]
  transfers between devices with their start and end apart: 20 -> 22, of which waited for: 18 -> 12; matrix products, arithmetic and copies ran while one was open for 6% -> 15% of each run, Pallas kernels for 0% -> 0%
where the time goes in v1:
time: 556 us; the launch traced here: 554 us
  waiting for transfers between devices  215 us (39%)
  blocking collectives  172 us (31%)
  matrix products  48.9 us (9%)
  local copies, waits for them, and re-layouts  44 us (8%)
  starting transfers between devices  30 us (5%)
  other arithmetic  28.4 us (5%)
  between operations  16.2 us (3%)
    reduce_scatter x3, waiting for transfers between devices, group_scatter(): lax.psum_scatter(partial_terms.astype(jnp.bfloat16), GROUP, scatter_dimen...  101 us
    all_gather x1, blocking collectives, shards(): lax.all_gather(jnp.concatenate((norm_vectors.reshape(-1), qkv_bias.reshap...  70.4 us
    all_gather x3, waiting for transfers between devices, group_gather(): return lax.all_gather(block, GROUP, axis=0, tiled=True)  63.6 us
    psum x1, blocking collectives, shards(): lax.psum(jnp.concatenate((grad_vectors.reshape(-1), ub_place.reshape(-1))...  40.2 us
    unnamed x93, local copies, waits for them, and re-layouts  25.1 us
    all_gather x1, waiting for transfers between devices, shards(): lax.all_gather(lax.all_to_all(down_weight.astype(bf16), 'col', 0, 1, tile...  23.7 us
    dot_general x4, matrix products, contract_cols(): lax.dot_general(left_side, right_side, (((1,), (1,)), ((), ())), preferre...  20 us
    all_gather x1, blocking collectives, shards(): lax.all_gather(lax.all_to_all(qkv_weight.astype(bf16).reshape(qkv_rows, n...  17.8 us
  transfers between devices with their start and end apart: 22, of which 12 were waited for; matrix products, arithmetic and copies ran while one was open for 15% of the time, Pallas kernels for 0%

profile of v1, /device:TPU:0, one launch (start us, length us, event | category | flops | bytes accessed | tf_op | source)
XLA Modules:
  0.0 553.9 jit_solution(5686297876662358540)
XLA Ops:
  11.2 4.2 all-to-all-start
  15.7 70.4 %all-gather.1 = bf16[32,1,416]{2,1,0:T(2,128)(2,1)S(1)} all-gather(bf16[1,1,416]{2,1,0:T(2,128)(2,1)S(1)} %maximum_bitcast_fusion), channel_id=1, replica_groups=mesh['dp'=4,'row'=2,'col'=4] {'col','row','dp'}, dimensions={0}, use_global_device_ids=true | all-gather | bytes 27456 | tf_op jit(solution)/shard_map/all_gather | solution.py:171
  87.0 14.7 %all_gather.31 = bf16[512,256]{1,0:T(8,128)(2,1)} all-gather(bf16[128,256]{1,0:T(8,128)(2,1)S(1)} %convert_element_type.183), channel_id=1, replica_groups=mesh['dp'=4,'row'=2,'col'=4] {'dp'}, dimensions={0}, use_global_device_ids=true | all-gather | bytes 327680 | tf_op jit(solution)/shard_map/all_gather | solution.py:155
  101.7 3.4 all-to-all-start.1
  105.3 17.8 %all-gather = bf16[4,256,1,384]{3,0,2,1:T(4,128)(2,1)S(1)} all-gather(bf16[4,64,1,384]{3,0,2,1:T(4,128)(2,1)S(1)} %copy.128), channel_id=2, replica_groups=mesh['dp'=4,'row'=2,'col'=4] {'dp'}, dimensions={1}, use_global_device_ids=true | all-gather | bytes 983040 | tf_op jit(solution)/shard_map/all_gather | solution.py:146
  124.1 2.8 add_convert_fusion
  132.6 2.1 convolution_convert_fusion.3
  134.9 8.8 %all_to_all.154 = bf16[4,128,256]{2,1,0:T(8,128)(2,1)S(1)} all-to-all(bf16[4,128,256]{2,1,0:T(8,128)(2,1)S(1)} %bitcast.202), channel_id=1, replica_groups=mesh['dp'=4,'row'=2,'col'=4] {'col'}, dimensions={0} | all-to-all | bytes 524288 | tf_op jit(solution)/shard_map/all_to_all | solution.py:165
  145.2 30.0 %reduce-scatter.11.cloned.1.call-done = bf16[128,1024]{1,0:T(8,128)(2,1)} async-done(((bf16[1024,1024]{1,0:T(8,128)(2,1)}), bf16[128,1024]{1,0:T(8,128)(2,1)}) %reduce-scatter.11.cloned.1.call-update) | async-done | bytes 262160 | tf_op jit(solution)/shard_map/reduce_scatter | solution.py:35
  179.1 3.4 all-to-all-start.3
  182.6 5.9 %all-to-all-done.3 = bf16[4,128,256]{2,1,0:T(8,128)(2,1)S(1)} async-done(((bf16[4,128,256]{2,1,0:T(8,128)(2,1)}), bf16[4,128,256]{2,1,0:T(8,128)(2,1)S(1)}, u32[]{:S(2)}, u32[]{:S(2)}) %all-to-all-start.3) | async-done | bytes 262176 | tf_op jit(solution)/shard_map/all_to_all | solution.py:168
  189.6 16.5 %all-gather.11.cloned.1.call-done = bf16[1024,1024]{1,0:T(8,128)(2,1)} async-done(((bf16[128,1024]{1,0:T(8,128)(2,1)}), bf16[1024,1024]{1,0:T(8,128)(2,1)}) %all-gather.11.cloned.1.call-update) | async-done | bytes 2097168 | tf_op jit(solution)/shard_map/all_gather | solution.py:27
  206.2 8.5 %multiply_convert_fusion.1 = (bf16[1024,512]{1,0:T(8,128)(2,1)S(1)}, f32[1024,512]{1,0:T(8,128)}, f32[1024,512]{1,0:T(8,128)}) fusion(f32[512]{0:T(512)S(1)} %bitcast.237, bf16[1024,1024]{1,0:T(8,128)(2,1)} %all-gather.11.cloned.1.call-done, bf16[512,1024]{0,1:T(8,128)(2,1)} %all-gather.13.cloned.1.call-done), kind=kOutput, calls=%fused_computation.13 | convolution fusion | flops 1108344832 | bytes 8390656 | tf_op jit(solution)/shard_map/dot_general | solution.py:61
  214.7 23.7 %all-gather.15.cloned.1.call-done = bf16[512,1024]{0,1:T(8,128)(2,1)} async-done(((bf16[128,1024]{0,1:T(8,128)(2,1)}), bf16[512,1024]{0,1:T(8,128)(2,1)}) %all-gather.15.cloned.1.call-update) | async-done | bytes 1048592 | tf_op jit(solution)/shard_map/all_gather | solution.py:167
  238.3 3.9 convolution_convert_fusion.2
  242.2 3.6 all-to-all-start.5
  246.1 6.0 %all-to-all-done.5 = bf16[8,128,128]{2,1,0:T(8,128)(2,1)S(1)} async-done(((bf16[8,128,128]{2,1,0:T(8,128)(2,1)}), bf16[8,128,128]{2,1,0:T(8,128)(2,1)S(1)}, u32[]{:S(2)}, u32[]{:S(2)}) %all-to-all-start.5) | async-done | bytes 262176 | tf_op jit(solution)/shard_map/all_to_all | solution.py:47
  252.3 29.6 %reduce-scatter.13.cloned.1.call-done = bf16[128,1024]{1,0:T(8,128)(2,1)} async-done(((bf16[1024,1024]{1,0:T(8,128)(2,1)}), bf16[128,1024]{1,0:T(8,128)(2,1)}) %reduce-scatter.13.cloned.1.call-update) | async-done | bytes 262160 | tf_op jit(solution)/shard_map/reduce_scatter | solution.py:35
  284.8 27.8 %all-gather.17.cloned.1.call-done = bf16[1024,1024]{1,0:T(8,128)(2,1)} async-done(((bf16[128,1024]{1,0:T(8,128)(2,1)}), bf16[1024,1024]{1,0:T(8,128)(2,1)}) %all-gather.17.cloned.1.call-update) | async-done | bytes 2097168 | tf_op jit(solution)/shard_map/all_gather | solution.py:27
  312.6 5.2 fusion.47
  318.8 2.6 convolution_convert_fusion.1
  321.4 41.3 %reduce-scatter.15.cloned.1.call-done = bf16[128,1024]{1,0:T(8,128)(2,1)} async-done(((bf16[1024,1024]{1,0:T(8,128)(2,1)}), bf16[128,1024]{1,0:T(8,128)(2,1)}) %reduce-scatter.15.cloned.1.call-update) | async-done | bytes 262160 | tf_op jit(solution)/shard_map/reduce_scatter | solution.py:35
  366.3 4.2 convolution_convert_fusion.5
  370.6 3.9 convolution_convert_fusion.4
  374.8 19.3 %all-gather.19.cloned.1.call-done = bf16[1024,1024]{1,0:T(8,128)(2,1)} async-done(((bf16[128,1024]{1,0:T(8,128)(2,1)}), bf16[1024,1024]{1,0:T(8,128)(2,1)}) %all-gather.19.cloned.1.call-update) | async-done | bytes 2097168 | tf_op jit(solution)/shard_map/all_gather | solution.py:27
  394.0 2.3 convolution_convert_fusion.8
  397.0 3.3 multiply_reduce_fusion
  408.1 2.5 copy.151
  410.5 2.1 copy.152
  413.2 9.1 %all_to_all.155 = bf16[128,4,256]{2,0,1:T(8,128)(2,1)} all-to-all(bf16[128,4,256]{2,0,1:T(8,128)(2,1)S(1)} %bitcast.214), channel_id=1, replica_groups=mesh['dp'=4,'row'=2,'col'=4] {'col'}, dimensions={1} | all-to-all | bytes 524288 | tf_op jit(solution)/shard_map/all_to_all | solution.py:293
  422.4 4.0 convolution_convert_fusion
  426.4 3.9 copy.169
  432.0 3.4 all-to-all-start.4
  437.1 4.7 all-to-all-done.4
  442.5 3.4 all-to-all-start.8
  445.9 5.6 %reduce-scatter.23.cloned.1.call-done = bf16[128,1024]{1,0:T(8,128)(2,1)} async-done(((bf16[512,1024]{1,0:T(8,128)(2,1)}), bf16[128,1024]{1,0:T(8,128)(2,1)}) %reduce-scatter.23.cloned.1.call-update) | async-done | bytes 262160 | tf_op jit(solution)/shard_map/reduce_scatter | solution.py:245
  453.2 4.0 all-to-all-start.9
  457.2 2.3 copy.156
  459.5 2.3 copy.150
  461.8 2.3 copy.154
  467.0 3.0 multiply_subtract_fusion.1
  471.7 40.2 %psum.15 = f32[10240]{0:T(1024)S(1)} all-reduce(f32[10240]{0:T(1024)S(1)} %pad_maximum_fusion.1), channel_id=1, replica_groups=mesh['dp'=4,'row'=2,'col'=4] {'col','row','dp'}, use_global_device_ids=true, to_apply=%region_28.29 | all-reduce | flops 10240 | bytes 81920 | tf_op jit(solution)/shard_map/psum | solution.py:316
  514.5 10.6 %psum.14 = f32[2,192]{1,0:T(2,128)S(1)} all-reduce(f32[2,192]{1,0:T(2,128)S(1)} %reshape.313), channel_id=1, replica_groups=mesh['dp'=4,'row'=2,'col'=4] {'dp'}, use_global_device_ids=true, to_apply=%region_20.21 | all-reduce | flops 384 | bytes 3072 | tf_op jit(solution)/shard_map/psum | solution.py:327
  525.8 3.5 all-to-all-start.6
  531.2 3.5 all-to-all-done.6
  535.0 3.2 multiply_subtract_fusion
  538.2 2.4 copy.162
  540.6 2.3 copy.163
  (218 shorter events, 54.3 us)
Async XLA Ops:
  8.0 7.4 %copy-start.26 = (f32[6,32]{1,0:T(8,128)S(1)}, f32[6,32]{1,0:T(8,128)}, u32[]{:S(2)}) copy-start(f32[6,32]{1,0:T(8,128)} %param.45) | copy-start | bytes 2308
  8.0 7.5 %copy-start.31 = (f32[2,48]{1,0:T(2,128)S(1)}, f32[2,48]{1,0:T(2,128)}, u32[]{:S(2)}) copy-start(f32[2,48]{1,0:T(2,128)} %param.39) | copy-start | bytes 1156
  8.0 7.6 %copy-start.35 = (f32[128]{0:T(128)S(1)}, f32[128]{0:T(128)}, u32[]{:S(2)}) copy-start(f32[128]{0:T(128)} %param.42) | copy-start | bytes 1540
  8.1 78.3 %copy-start.30 = (s32[1024]{0:T(1024)S(1)}, s32[1024]{0:T(1024)}, u32[]{:S(2)}) copy-start(s32[1024]{0:T(1024)} %param.25) | copy-start | bytes 12292
  8.1 78.9 %copy-start.24 = (f32[128,256]{1,0:T(8,128)S(1)}, f32[128,256]{1,0:T(8,128)}, u32[]{:S(2)}) copy-start(f32[128,256]{1,0:T(8,128)} %param.30) | copy-start | bytes 393220
  8.1 115.4 %all-gather.9.cloned.1.call-start = ((), (), s32[]{:S(2)}) async-start(), calls=%async_computation.18 | async-start | bytes 2359296 | tf_op jit(solution)/shard_map/all_gather | solution.py:31
  11.2 90.5 %all-to-all-start = ((bf16[64,4,384]{2,0,1:T(8,128)(2,1)}), bf16[64,4,384]{2,0,1:T(8,128)(2,1)S(1)}, u32[]{:S(2)}, u32[]{:S(2)}) async-start(bf16[64,4,384]{2,0,1:T(8,128)(2,1)} %copy.127), calls=%async_computation | async-start | bytes 393216 | tf_op jit(solution)/shard_map/all_to_all | solution.py:147
  101.7 21.6 %all-to-all-start.1 = ((bf16[4,128,256]{2,1,0:T(8,128)(2,1)}), bf16[4,128,256]{2,1,0:T(8,128)(2,1)S(1)}, u32[]{:S(2)}, u32[]{:S(2)}) async-start(bf16[4,128,256]{2,1,0:T(8,128)(2,1)} %bitcast.12), calls=%async_computation.1 | async-start | bytes 524288 | tf_op jit(solution)/shard_map/all_to_all | solution.py:154
  105.1 70.1 %reduce-scatter.11.cloned.1.call-start = ((), (), s32[]{:S(2)}) async-start(), calls=%async_computation.19 | async-start | bytes 2359296 | tf_op jit(solution)/shard_map/reduce_scatter | solution.py:35
  134.7 43.6 %copy-start.10 = (f32[512,256]{1,0:T(8,128)S(1)}, f32[512,256]{1,0:T(8,128)}, u32[]{:S(2)}) copy-start(f32[512,256]{1,0:T(8,128)} %param.36) | copy-start | bytes 1572868
  134.7 54.9 %all-gather.13.cloned.1.call-start = ((), (), s32[]{:S(2)}) async-start(), calls=%async_computation.21 | async-start | bytes 1310720 | tf_op jit(solution)/shard_map/all_gather | solution.py:164
  144.5 61.6 %all-gather.11.cloned.1.call-start = ((), (), s32[]{:S(2)}) async-start(), calls=%async_computation.20 | async-start | bytes 2359296 | tf_op jit(solution)/shard_map/all_gather | solution.py:27
  179.1 9.4 %all-to-all-start.3 = ((bf16[4,128,256]{2,1,0:T(8,128)(2,1)}), bf16[4,128,256]{2,1,0:T(8,128)(2,1)S(1)}, u32[]{:S(2)}, u32[]{:S(2)}) async-start(bf16[4,128,256]{2,1,0:T(8,128)(2,1)} %bitcast.22), calls=%async_computation.4 | async-start | bytes 524288 | tf_op jit(solution)/shard_map/all_to_all | solution.py:168
  182.5 55.9 %all-gather.15.cloned.1.call-start = ((), (), s32[]{:S(2)}) async-start(), calls=%async_computation.22 | async-start | bytes 1310720 | tf_op jit(solution)/shard_map/all_gather | solution.py:167
  189.3 92.6 %reduce-scatter.13.cloned.1.call-start = ((), (), s32[]{:S(2)}) async-start(), calls=%async_computation.23 | async-start | bytes 2359296 | tf_op jit(solution)/shard_map/reduce_scatter | solution.py:35
  242.2 39.7 %copy-start.3 = (bf16[128,1024]{1,0:T(8,128)(2,1)S(1)}, bf16[128,1024]{1,0:T(8,128)(2,1)}, u32[]{:S(2)}) copy-start(bf16[128,1024]{1,0:T(8,128)(2,1)} %reduce-scatter.11.cloned.1.call-done) | copy-start | bytes 786436
  242.2 9.9 %all-to-all-start.5 = ((bf16[8,128,128]{2,1,0:T(8,128)(2,1)}), bf16[8,128,128]{2,1,0:T(8,128)(2,1)S(1)}, u32[]{:S(2)}, u32[]{:S(2)}) async-start(bf16[8,128,128]{2,1,0:T(8,128)(2,1)} %bitcast.27), calls=%async_computation.7 | async-start | bytes 524288 | tf_op jit(solution)/shard_map/all_to_all | solution.py:47
  245.8 66.8 %all-gather.17.cloned.1.call-start = ((), (), s32[]{:S(2)}) async-start(), calls=%async_computation.24 | async-start | bytes 2359296 | tf_op jit(solution)/shard_map/all_gather | solution.py:27
  284.7 78.0 %reduce-scatter.15.cloned.1.call-start = ((), (), s32[]{:S(2)}) async-start(), calls=%async_computation.25 | async-start | bytes 2359296 | tf_op jit(solution)/shard_map/reduce_scatter | solution.py:35
  312.6 6.2 %copy-start.39 = (bf16[512,1024]{0,1:T(8,128)(2,1)S(1)}, bf16[512,1024]{0,1:T(8,128)(2,1)}, u32[]{:S(2)}) copy-start(bf16[512,1024]{0,1:T(8,128)(2,1)} %all-gather.13.cloned.1.call-done) | copy-start | bytes 3145732
  321.4 72.6 %all-gather.19.cloned.1.call-start = ((), (), s32[]{:S(2)}) async-start(), calls=%async_computation.26 | async-start | bytes 2359296 | tf_op jit(solution)/shard_map/all_gather | solution.py:27
  366.2 69.2 %reduce-scatter.21.cloned.1.call-start = ((), (), s32[]{:S(2)}) async-start(), calls=%async_computation.29 | async-start | bytes 1310720 | tf_op jit(solution)/shard_map/reduce_scatter | solution.py:248
  370.5 81.0 %reduce-scatter.23.cloned.1.call-start = ((), (), s32[]{:S(2)}) async-start(), calls=%async_computation.30 | async-start | bytes 1310720 | tf_op jit(solution)/shard_map/reduce_scatter | solution.py:245
  374.5 151.3 %reduce-scatter.17.cloned.1.call-start = ((), (), s32[]{:S(2)}) async-start(), calls=%async_computation.27 | async-start | bytes 983040 | tf_op jit(solution)/shard_map/reduce_scatter | solution.py:279
  397.0 3.5 copy-start.1
  408.1 4.6 copy-start.2
  412.7 116.7 %reduce-scatter.19.cloned.1.call-start = ((), (), s32[]{:S(2)}) async-start(), calls=%async_computation.28 | async-start | bytes 327680 | tf_op jit(solution)/shard_map/reduce_scatter | solution.py:292
  422.3 121.7 %reduce-scatter.25.cloned.1.call-start = ((), (), s32[]{:S(2)}) async-start(), calls=%async_computation.31 | async-start | bytes 2359296
  432.0 9.8 %all-to-all-start.4 = ((bf16[128,8,128]{2,0,1:T(8,128)(2,1)}), bf16[128,8,128]{2,0,1:T(8,128)(2,1)S(1)}, u32[]{:S(2)}, u32[]{:S(2)}) async-start(bf16[128,8,128]{2,0,1:T(8,128)(2,1)} %bitcast.211), calls=%async_computation.6 | async-start | bytes 524288 | tf_op jit(solution)/shard_map/all_to_all | solution.py:51
  442.5 10.7 %all-to-all-start.8 = ((bf16[128,4,256]{2,0,1:T(8,128)(2,1)}), bf16[128,4,256]{2,0,1:T(8,128)(2,1)S(1)}, u32[]{:S(2)}, u32[]{:S(2)}) async-start(bf16[128,4,256]{2,0,1:T(8,128)(2,1)} %bitcast.210), calls=%async_computation.14 | async-start | bytes 524288 | tf_op jit(solution)/shard_map/all_to_all | solution.py:337
  453.2 13.8 %all-to-all-start.9 = ((bf16[128,4,256]{2,0,1:T(8,128)(2,1)}), bf16[128,4,256]{2,0,1:T(8,128)(2,1)}, u32[]{:S(2)}, u32[]{:S(2)}) async-start(bf16[128,4,256]{2,0,1:T(8,128)(2,1)} %bitcast.206), calls=%async_computation.16 | async-start | bytes 524288 | tf_op jit(solution)/shard_map/all_to_all | solution.py:338
  467.0 3.0 copy-start.8
  467.0 3.0 copy-start.9
  467.0 3.0 copy-start.22
  470.1 41.8 %copy-start.36 = (f32[128]{0:T(128)S(1)}, f32[128]{0:T(128)}, u32[]{:S(2)}) copy-start(f32[128]{0:T(128)} %param.42) | copy-start | bytes 1540
  470.1 41.8 %copy-start.37 = (f32[128]{0:T(128)S(1)}, f32[128]{0:T(128)}, u32[]{:S(2)}) copy-start(f32[128]{0:T(128)} %param.43) | copy-start | bytes 1540
  470.1 41.8 %copy-start.38 = (f32[128]{0:T(128)S(1)}, f32[128]{0:T(128)}, u32[]{:S(2)}) copy-start(f32[128]{0:T(128)} %param.44) | copy-start | bytes 1540
  470.1 42.5 %copy-start.27 = (f32[6,32]{1,0:T(8,128)S(1)}, f32[6,32]{1,0:T(8,128)}, u32[]{:S(2)}) copy-start(f32[6,32]{1,0:T(8,128)} %param.45) | copy-start | bytes 2308
  470.1 42.4 %copy-start.28 = (f32[6,32]{1,0:T(8,128)S(1)}, f32[6,32]{1,0:T(8,128)}, u32[]{:S(2)}) copy-start(f32[6,32]{1,0:T(8,128)} %param.46) | copy-start | bytes 2308
  470.1 42.4 %copy-start.29 = (f32[6,32]{1,0:T(8,128)S(1)}, f32[6,32]{1,0:T(8,128)}, u32[]{:S(2)}) copy-start(f32[6,32]{1,0:T(8,128)} %param.47) | copy-start | bytes 2308
  470.1 55.0 %copy-start.32 = (f32[2,48]{1,0:T(2,128)S(1)}, f32[2,48]{1,0:T(2,128)}, u32[]{:S(2)}) copy-start(f32[2,48]{1,0:T(2,128)} %param.39) | copy-start | bytes 1156
  470.1 55.0 %copy-start.33 = (f32[2,48]{1,0:T(2,128)S(1)}, f32[2,48]{1,0:T(2,128)}, u32[]{:S(2)}) copy-start(f32[2,48]{1,0:T(2,128)} %param.40) | copy-start | bytes 1156
  470.1 55.0 %copy-start.34 = (f32[2,48]{1,0:T(2,128)S(1)}, f32[2,48]{1,0:T(2,128)}, u32[]{:S(2)}) copy-start(f32[2,48]{1,0:T(2,128)} %param.41) | copy-start | bytes 1156
  471.6 57.8 %copy-start.25 = (f32[128,256]{1,0:T(8,128)S(1)}, f32[128,256]{1,0:T(8,128)}, u32[]{:S(2)}) copy-start(f32[128,256]{1,0:T(8,128)} %param.30) | copy-start | bytes 393220
  514.4 20.6 %copy-start.5 = (f32[64,8,3,64]{0,3,2,1:T(8,128)S(1)}, f32[64,8,3,64]{0,3,2,1:T(8,128)}, u32[]{:S(2)}) copy-start(f32[64,8,3,64]{0,3,2,1:T(8,128)} %copy.156) | copy-start | bytes 1179652
  525.8 8.9 %all-to-all-start.6 = ((bf16[4,64,384]{2,1,0:T(8,128)(2,1)}), bf16[4,64,384]{2,1,0:T(8,128)(2,1)S(1)}, u32[]{:S(2)}, u32[]{:S(2)}) async-start(bf16[4,64,384]{2,1,0:T(8,128)(2,1)} %bitcast.224), calls=%async_computation.10 | async-start | bytes 393216 | tf_op jit(solution)/shard_map/all_to_all | solution.py:333
  538.2 4.7 copy-start.6
  540.6 5.5 copy-start.12
  (14 other events, 18.5 us)
Sparse Core Ops, SparseCore 0:
  10.8 30.9 all-gather.8
  134.8 40.2 reduce-scatter.10
  242.4 39.5 reduce-scatter.12
  321.5 41.1 reduce-scatter.14
Sparse Core Ops, SparseCore 1:
  144.6 27.9 all-gather.12
  178.4 27.7 all-gather.10
  208.2 30.1 all-gather.14
  284.8 27.7 all-gather.16
  366.3 27.7 all-gather.18
  396.5 27.1 reduce-scatter.20
  425.8 25.7 reduce-scatter.22
  454.4 21.6 reduce-scatter.16
  478.2 19.2 reduce-scatter.18
  500.7 39.6 reduce-scatter.24

commit v2 on v1

--- a/solution.py
+++ b/solution.py
@@ -143,13 +143,19 @@
     d_col = D // n_col
     ff_own = up_weight.shape[1] // n_col
     ff_local = ff_own * n_dp
-    w_qkv = lax.all_gather(
-        lax.all_to_all(
-            qkv_weight.astype(bf16).reshape(qkv_rows, n_col, width), "col", 1, 0, tiled=True
-        ).reshape(n_col, qkv_rows, width),
-        "dp",
-        axis=1,
-    ).reshape(D, width)
+    w_qkv = (
+        lax.all_gather(
+            lax.all_to_all(
+                qkv_weight.astype(bf16).reshape(qkv_rows, n_col, width), "col", 1, 0, tiled=True
+            ).reshape(n_col * qkv_rows, width),
+            "dp",
+            axis=0,
+            tiled=True,
+        )
+        .reshape(n_dp, n_col, qkv_rows, width)
+        .transpose(1, 0, 2, 3)
+        .reshape(D, width)
+    )
     w_out = (
         lax.all_to_all(
             lax.all_gather(out_weight.astype(bf16), "dp", axis=0, tiled=True).reshape(
@@ -313,22 +319,28 @@
         grad_up_bias.reshape(1, n_dp, 1, ff_own),
         (at_row, 0, at_col, 0),
     )
-    sums = lax.psum(jnp.concatenate((grad_vectors.reshape(-1), ub_place.reshape(-1))), ("col", "row", "dp"))
-    grad_vectors = lax.dynamic_slice_in_dim(
-        sums[: 6 * D].reshape(6, D), (at_group * n_dp + at_dp) * n_vec, n_vec, 1
-    )
-    grad_up_bias = lax.dynamic_slice_in_dim(
-        sums[6 * D :],
-        ((at_row * n_col + at_col) * n_dp + at_dp) * up_bias.shape[0],
-        up_bias.shape[0],
-        0,
-    )
-    grad_qkv_bias = lax.dynamic_slice_in_dim(
-        lax.psum(grad_qkv_bias, "dp").reshape(heads_local, -1),
-        at_dp * qkv_bias.shape[1],
-        qkv_bias.shape[1],
-        1,
-    )
+    ub_blocks = (
+        ub_place.reshape(n_row, n_col, n_dp, -1).transpose(1, 0, 2, 3).reshape(-1, up_bias.shape[0])
+    )
+    qb_blocks = lax.dynamic_update_slice(
+        jnp.zeros((n_col * n_row, n_dp, qb_size), f32),
+        grad_qkv_bias.reshape(heads_local, n_dp, -1).transpose(1, 0, 2).reshape(1, n_dp, qb_size),
+        (at_group, 0, 0),
+    ).reshape(-1, qb_size)
+    vec_blocks = grad_vectors.reshape(6, -1, n_vec).transpose(1, 0, 2).reshape(-1, vec_size)
+    sums = jnp.sum(
+        lax.all_to_all(
+            jnp.concatenate((vec_blocks, qb_blocks, ub_blocks), axis=1),
+            ("col", "row", "dp"),
+            0,
+            0,
+            tiled=True,
+        ),
+        axis=0,
+    )
+    grad_vectors = sums[:vec_size].reshape(norm_vectors.shape)
+    grad_qkv_bias = sums[vec_size : vec_size + qb_size].reshape(qkv_bias.shape)
+    grad_up_bias = sums[vec_size + qb_size :]
     gradients = (
         lax.all_to_all(grad_qkv_weight, "col", 0, 2, tiled=True)
         .reshape(qkv_weight.shape)

time: 556 us -> 552 us (level)
  blocking collectives: 172 us -> 121 us
  waiting for transfers between devices: 215 us -> 253 us
  starting transfers between devices: 30 us -> 35.7 us
    psum x2 -> x0, blocking collectives: 50.8 us -> none  [the longest x1 40.2 us: shards(): lax.psum(jnp.concatenate((grad_vectors.reshape(-1), ub_place.reshape(-1))...]
    unnamed x15, waiting for transfers between devices: 0.9 us -> 32.4 us
    reduce_scatter x1, waiting for transfers between devices: 0.01 us -> 11.5 us  [shards(): lax.psum_scatter(lax.all_to_all(contract_rows(attended, grad_one_rows).as...]
    all_to_all x0 -> x1, starting transfers between devices: none -> 5.85 us  [shards(): lax.all_to_all(jnp.concatenate((vec_blocks, qb_blocks, ub_blocks), axis=1...]
    reduce_scatter x1, waiting for transfers between devices: 5.59 us -> 0.02 us  [shards(): lax.psum_scatter(contract_rows(act_rows, grad_two_rows).astype(bf16), 'dp...]
    unnamed x93 -> x87, local copies, waits for them, and re-layouts: 25.1 us -> 25.1 us
  transfers between devices with their start and end apart: 22 -> 23, of which waited for: 12 -> 13; matrix products, arithmetic and copies ran while one was open for 15% -> 16% of each run, Pallas kernels for 0% -> 0%
where the time goes in v2:
time: 552 us; the launch traced here: 550 us
  waiting for transfers between devices  253 us (46%)
  blocking collectives  121 us (22%)
  matrix products  48.9 us (9%)
  local copies, waits for them, and re-layouts  45.6 us (8%)
  starting transfers between devices  35.7 us (6%)
  other arithmetic  29.6 us (5%)
  between operations  16.1 us (3%)
    reduce_scatter x3, waiting for transfers between devices, group_scatter(): lax.psum_scatter(partial_terms.astype(jnp.bfloat16), GROUP, scatter_dimen...  101 us
    all_gather x1, blocking collectives, shards(): lax.all_gather(jnp.concatenate((norm_vectors.reshape(-1), qkv_bias.reshap...  70.4 us
    all_gather x3, waiting for transfers between devices, group_gather(): return lax.all_gather(block, GROUP, axis=0, tiled=True)  63.6 us
    unnamed x15, waiting for transfers between devices  32.4 us
    unnamed x87, local copies, waits for them, and re-layouts  25.1 us
    all_gather x1, waiting for transfers between devices, shards(): lax.all_gather(lax.all_to_all(down_weight.astype(bf16), 'col', 0, 1, tile...  23.7 us
    dot_general x4, matrix products, contract_cols(): lax.dot_general(left_side, right_side, (((1,), (1,)), ((), ())), preferre...  20 us
    all_gather x1, blocking collectives, shards(): lax.all_gather(lax.all_to_all(qkv_weight.astype(bf16).reshape(qkv_rows, n...  17.8 us
  transfers between devices with their start and end apart: 23, of which 13 were waited for; matrix products, arithmetic and copies ran while one was open for 16% of the time, Pallas kernels for 0%

profile of v2, /device:TPU:0, one launch (start us, length us, event | category | flops | bytes accessed | tf_op | source)
XLA Modules:
  0.0 549.7 jit_solution(629811033751891943)
XLA Ops:
  11.2 4.2 all-to-all-start
  15.7 70.4 %all-gather = bf16[32,1,416]{2,1,0:T(2,128)(2,1)S(1)} all-gather(bf16[1,1,416]{2,1,0:T(2,128)(2,1)S(1)} %maximum_bitcast_fusion.1), channel_id=1, replica_groups=mesh['dp'=4,'row'=2,'col'=4] {'col','row','dp'}, dimensions={0}, use_global_device_ids=true | all-gather | bytes 27456 | tf_op jit(solution)/shard_map/all_gather | solution.py:177
  87.0 14.7 %all_gather.31 = bf16[512,256]{1,0:T(8,128)(2,1)} all-gather(bf16[128,256]{1,0:T(8,128)(2,1)S(1)} %convert_element_type.183), channel_id=1, replica_groups=mesh['dp'=4,'row'=2,'col'=4] {'dp'}, dimensions={0}, use_global_device_ids=true | all-gather | bytes 327680 | tf_op jit(solution)/shard_map/all_gather | solution.py:161
  101.7 3.4 all-to-all-start.1
  105.1 17.8 %all_gather.29 = bf16[1024,384]{1,0:T(8,128)(2,1)S(1)} all-gather(bf16[256,384]{1,0:T(8,128)(2,1)S(1)} %bitcast.226), channel_id=1, replica_groups=mesh['dp'=4,'row'=2,'col'=4] {'dp'}, dimensions={0}, use_global_device_ids=true | all-gather | bytes 983040 | tf_op jit(solution)/shard_map/all_gather | solution.py:147
  123.9 2.8 add_convert_fusion
  134.7 8.8 %all_to_all.163 = bf16[4,128,256]{2,1,0:T(8,128)(2,1)S(1)} all-to-all(bf16[4,128,256]{2,1,0:T(8,128)(2,1)S(1)} %bitcast.209), channel_id=1, replica_groups=mesh['dp'=4,'row'=2,'col'=4] {'col'}, dimensions={0} | all-to-all | bytes 524288 | tf_op jit(solution)/shard_map/all_to_all | solution.py:171
  145.0 30.0 %reduce-scatter.11.cloned.1.call-done = bf16[128,1024]{1,0:T(8,128)(2,1)} async-done(((bf16[1024,1024]{1,0:T(8,128)(2,1)}), bf16[128,1024]{1,0:T(8,128)(2,1)}) %reduce-scatter.11.cloned.1.call-update) | async-done | bytes 262160 | tf_op jit(solution)/shard_map/reduce_scatter | solution.py:35
  178.9 3.4 all-to-all-start.3
  182.4 5.9 %all-to-all-done.3 = bf16[4,128,256]{2,1,0:T(8,128)(2,1)S(1)} async-done(((bf16[4,128,256]{2,1,0:T(8,128)(2,1)}), bf16[4,128,256]{2,1,0:T(8,128)(2,1)S(1)}, u32[]{:S(2)}, u32[]{:S(2)}) %all-to-all-start.3) | async-done | bytes 262176 | tf_op jit(solution)/shard_map/all_to_all | solution.py:174
  189.4 16.5 %all-gather.10.cloned.1.call-done = bf16[1024,1024]{1,0:T(8,128)(2,1)} async-done(((bf16[128,1024]{1,0:T(8,128)(2,1)}), bf16[1024,1024]{1,0:T(8,128)(2,1)}) %all-gather.10.cloned.1.call-update) | async-done | bytes 2097168 | tf_op jit(solution)/shard_map/all_gather | solution.py:27
  206.0 8.5 %multiply_convert_fusion.1 = (bf16[1024,512]{1,0:T(8,128)(2,1)S(1)}, f32[1024,512]{1,0:T(8,128)}, f32[1024,512]{1,0:T(8,128)}) fusion(f32[512]{0:T(512)S(1)} %bitcast.241, bf16[1024,1024]{1,0:T(8,128)(2,1)} %all-gather.10.cloned.1.call-done, bf16[512,1024]{0,1:T(8,128)(2,1)} %all-gather.12.cloned.1.call-done), kind=kOutput, calls=%fused_computation.13 | convolution fusion | flops 1108344832 | bytes 8390656 | tf_op jit(solution)/shard_map/dot_general | solution.py:61
  214.5 23.7 %all-gather.14.cloned.1.call-done = bf16[512,1024]{0,1:T(8,128)(2,1)} async-done(((bf16[128,1024]{0,1:T(8,128)(2,1)}), bf16[512,1024]{0,1:T(8,128)(2,1)}) %all-gather.14.cloned.1.call-update) | async-done | bytes 1048592 | tf_op jit(solution)/shard_map/all_gather | solution.py:173
  238.2 3.9 convolution_convert_fusion.2
  242.1 3.6 all-to-all-start.5
  246.0 6.0 %all-to-all-done.5 = bf16[8,128,128]{2,1,0:T(8,128)(2,1)S(1)} async-done(((bf16[8,128,128]{2,1,0:T(8,128)(2,1)}), bf16[8,128,128]{2,1,0:T(8,128)(2,1)S(1)}, u32[]{:S(2)}, u32[]{:S(2)}) %all-to-all-start.5) | async-done | bytes 262176 | tf_op jit(solution)/shard_map/all_to_all | solution.py:47
  252.2 29.6 %reduce-scatter.13.cloned.1.call-done = bf16[128,1024]{1,0:T(8,128)(2,1)} async-done(((bf16[1024,1024]{1,0:T(8,128)(2,1)}), bf16[128,1024]{1,0:T(8,128)(2,1)}) %reduce-scatter.13.cloned.1.call-update) | async-done | bytes 262160 | tf_op jit(solution)/shard_map/reduce_scatter | solution.py:35
  284.6 27.8 %all-gather.16.cloned.1.call-done = bf16[1024,1024]{1,0:T(8,128)(2,1)} async-done(((bf16[128,1024]{1,0:T(8,128)(2,1)}), bf16[1024,1024]{1,0:T(8,128)(2,1)}) %all-gather.16.cloned.1.call-update) | async-done | bytes 2097168 | tf_op jit(solution)/shard_map/all_gather | solution.py:27
  312.4 5.2 fusion.48
  318.6 2.6 convolution_convert_fusion.1
  321.2 41.3 %reduce-scatter.15.cloned.1.call-done = bf16[128,1024]{1,0:T(8,128)(2,1)} async-done(((bf16[1024,1024]{1,0:T(8,128)(2,1)}), bf16[128,1024]{1,0:T(8,128)(2,1)}) %reduce-scatter.15.cloned.1.call-update) | async-done | bytes 262160 | tf_op jit(solution)/shard_map/reduce_scatter | solution.py:35
  366.1 4.2 convolution_convert_fusion.5
  370.4 3.9 convolution_convert_fusion.4
  374.6 19.3 %all-gather.18.cloned.1.call-done = bf16[1024,1024]{1,0:T(8,128)(2,1)} async-done(((bf16[128,1024]{1,0:T(8,128)(2,1)}), bf16[1024,1024]{1,0:T(8,128)(2,1)}) %all-gather.18.cloned.1.call-update) | async-done | bytes 2097168 | tf_op jit(solution)/shard_map/all_gather | solution.py:27
  393.8 2.3 convolution_convert_fusion.8
  396.8 3.3 multiply_reduce_fusion
  407.8 2.5 copy.153
  410.3 2.1 copy.154
  413.0 9.1 %all_to_all.164 = bf16[128,4,256]{2,0,1:T(8,128)(2,1)} all-to-all(bf16[128,4,256]{2,0,1:T(8,128)(2,1)S(1)} %bitcast.221), channel_id=1, replica_groups=mesh['dp'=4,'row'=2,'col'=4] {'col'}, dimensions={1} | all-to-all | bytes 524288 | tf_op jit(solution)/shard_map/all_to_all | solution.py:299
  422.1 4.0 convolution_convert_fusion
  426.1 4.0 copy.173
  431.8 3.4 all-to-all-start.4
  436.9 4.7 all-to-all-done.4
  442.3 3.4 all-to-all-start.8
  445.7 2.3 copy.158
  448.0 2.3 copy.152
  450.3 2.3 copy.156
  454.5 4.0 all-to-all-start.9
  461.4 2.9 multiply_subtract_fusion.2
  467.3 5.8 %all-to-all-start.10 = ((f32[32,1,416]{2,1,0:T(1,128)}), f32[32,1,416]{2,1,0:T(1,128)S(1)}, u32[]{:S(2)}, u32[]{:S(2)}) async-start(f32[32,1,416]{2,1,0:T(1,128)} %copy.165), calls=%async_computation.17 | async-start | bytes 131072 | tf_op jit(solution)/shard_map/all_to_all | solution.py:332
  473.2 2.8 multiply_subtract_fusion.1
  476.0 4.2 all-to-all-done.10
  482.3 3.4 all-to-all-start.6
  485.7 11.5 %reduce-scatter.19.cloned.1.call-done = bf16[128,256]{1,0:T(8,128)(2,1)} async-done(((bf16[512,256]{1,0:T(8,128)(2,1)}), bf16[128,256]{1,0:T(8,128)(2,1)}) %reduce-scatter.19.cloned.1.call-update) | async-done | bytes 65552 | tf_op jit(solution)/shard_map/reduce_scatter | solution.py:298
  499.3 3.2 multiply_subtract_fusion
  502.5 2.4 copy.166
  504.8 2.4 copy.167
  508.3 31.5 %reduce-scatter.25.cloned.1.call-done = bf16[128,1024]{1,0:T(8,128)(2,1)} async-done(((bf16[1024,1024]{1,0:T(8,128)(2,1)}), bf16[128,1024]{1,0:T(8,128)(2,1)}) %reduce-scatter.25.cloned.1.call-update) | async-done | bytes 262160
  (224 shorter events, 56.4 us)
Async XLA Ops:
  8.0 7.4 %copy-start.23 = (f32[6,32]{1,0:T(8,128)S(1)}, f32[6,32]{1,0:T(8,128)}, u32[]{:S(2)}) copy-start(f32[6,32]{1,0:T(8,128)} %param.45) | copy-start | bytes 2308
  8.0 7.5 %copy-start.28 = (f32[2,48]{1,0:T(2,128)S(1)}, f32[2,48]{1,0:T(2,128)}, u32[]{:S(2)}) copy-start(f32[2,48]{1,0:T(2,128)} %param.39) | copy-start | bytes 1156
  8.0 7.6 %copy-start.32 = (f32[128]{0:T(128)S(1)}, f32[128]{0:T(128)}, u32[]{:S(2)}) copy-start(f32[128]{0:T(128)} %param.42) | copy-start | bytes 1540
  8.1 78.3 %copy-start.27 = (s32[1024]{0:T(1024)S(1)}, s32[1024]{0:T(1024)}, u32[]{:S(2)}) copy-start(s32[1024]{0:T(1024)} %param.25) | copy-start | bytes 12292
  8.1 78.9 %copy-start.20 = (f32[128,256]{1,0:T(8,128)S(1)}, f32[128,256]{1,0:T(8,128)}, u32[]{:S(2)}) copy-start(f32[128,256]{1,0:T(8,128)} %param.30) | copy-start | bytes 393220
  8.1 115.2 %all-gather.8.cloned.1.call-start = ((), (), s32[]{:S(2)}) async-start(), calls=%async_computation.19 | async-start | bytes 2359296 | tf_op jit(solution)/shard_map/all_gather | solution.py:31
  11.2 90.5 %all-to-all-start = ((bf16[64,4,384]{2,0,1:T(8,128)(2,1)}), bf16[64,4,384]{2,0,1:T(8,128)(2,1)S(1)}, u32[]{:S(2)}, u32[]{:S(2)}) async-start(bf16[64,4,384]{2,0,1:T(8,128)(2,1)} %copy.130), calls=%async_computation | async-start | bytes 393216 | tf_op jit(solution)/shard_map/all_to_all | solution.py:148
  101.7 21.4 %all-to-all-start.1 = ((bf16[4,128,256]{2,1,0:T(8,128)(2,1)}), bf16[4,128,256]{2,1,0:T(8,128)(2,1)S(1)}, u32[]{:S(2)}, u32[]{:S(2)}) async-start(bf16[4,128,256]{2,1,0:T(8,128)(2,1)} %bitcast.15), calls=%async_computation.1 | async-start | bytes 524288 | tf_op jit(solution)/shard_map/all_to_all | solution.py:160
  105.1 69.9 %reduce-scatter.11.cloned.1.call-start = ((), (), s32[]{:S(2)}) async-start(), calls=%async_computation.20 | async-start | bytes 2359296 | tf_op jit(solution)/shard_map/reduce_scatter | solution.py:35
  132.4 2.2 copy-start.7
  134.5 43.6 %copy-start.8 = (f32[512,256]{1,0:T(8,128)S(1)}, f32[512,256]{1,0:T(8,128)}, u32[]{:S(2)}) copy-start(f32[512,256]{1,0:T(8,128)} %param.36) | copy-start | bytes 1572868
  134.5 54.9 %all-gather.12.cloned.1.call-start = ((), (), s32[]{:S(2)}) async-start(), calls=%async_computation.22 | async-start | bytes 1310720 | tf_op jit(solution)/shard_map/all_gather | solution.py:170
  144.3 61.6 %all-gather.10.cloned.1.call-start = ((), (), s32[]{:S(2)}) async-start(), calls=%async_computation.21 | async-start | bytes 2359296 | tf_op jit(solution)/shard_map/all_gather | solution.py:27
  178.9 9.4 %all-to-all-start.3 = ((bf16[4,128,256]{2,1,0:T(8,128)(2,1)}), bf16[4,128,256]{2,1,0:T(8,128)(2,1)S(1)}, u32[]{:S(2)}, u32[]{:S(2)}) async-start(bf16[4,128,256]{2,1,0:T(8,128)(2,1)} %bitcast.25), calls=%async_computation.4 | async-start | bytes 524288 | tf_op jit(solution)/shard_map/all_to_all | solution.py:174
  182.3 55.9 %all-gather.14.cloned.1.call-start = ((), (), s32[]{:S(2)}) async-start(), calls=%async_computation.23 | async-start | bytes 1310720 | tf_op jit(solution)/shard_map/all_gather | solution.py:173
  189.2 92.6 %reduce-scatter.13.cloned.1.call-start = ((), (), s32[]{:S(2)}) async-start(), calls=%async_computation.24 | async-start | bytes 2359296 | tf_op jit(solution)/shard_map/reduce_scatter | solution.py:35
  242.0 39.7 %copy-start.3 = (bf16[128,1024]{1,0:T(8,128)(2,1)S(1)}, bf16[128,1024]{1,0:T(8,128)(2,1)}, u32[]{:S(2)}) copy-start(bf16[128,1024]{1,0:T(8,128)(2,1)} %reduce-scatter.11.cloned.1.call-done) | copy-start | bytes 786436
  242.1 9.9 %all-to-all-start.5 = ((bf16[8,128,128]{2,1,0:T(8,128)(2,1)}), bf16[8,128,128]{2,1,0:T(8,128)(2,1)S(1)}, u32[]{:S(2)}, u32[]{:S(2)}) async-start(bf16[8,128,128]{2,1,0:T(8,128)(2,1)} %bitcast.30), calls=%async_computation.7 | async-start | bytes 524288 | tf_op jit(solution)/shard_map/all_to_all | solution.py:47
  245.6 66.8 %all-gather.16.cloned.1.call-start = ((), (), s32[]{:S(2)}) async-start(), calls=%async_computation.25 | async-start | bytes 2359296 | tf_op jit(solution)/shard_map/all_gather | solution.py:27
  284.6 78.0 %reduce-scatter.15.cloned.1.call-start = ((), (), s32[]{:S(2)}) async-start(), calls=%async_computation.26 | async-start | bytes 2359296 | tf_op jit(solution)/shard_map/reduce_scatter | solution.py:35
  312.4 6.2 %copy-start.36 = (bf16[512,1024]{0,1:T(8,128)(2,1)S(1)}, bf16[512,1024]{0,1:T(8,128)(2,1)}, u32[]{:S(2)}) copy-start(bf16[512,1024]{0,1:T(8,128)(2,1)} %all-gather.12.cloned.1.call-done) | copy-start | bytes 3145732
  321.2 72.6 %all-gather.18.cloned.1.call-start = ((), (), s32[]{:S(2)}) async-start(), calls=%async_computation.27 | async-start | bytes 2359296 | tf_op jit(solution)/shard_map/all_gather | solution.py:27
  366.0 69.2 %reduce-scatter.21.cloned.1.call-start = ((), (), s32[]{:S(2)}) async-start(), calls=%async_computation.30 | async-start | bytes 1310720 | tf_op jit(solution)/shard_map/reduce_scatter | solution.py:254
  370.3 82.5 %reduce-scatter.23.cloned.1.call-start = ((), (), s32[]{:S(2)}) async-start(), calls=%async_computation.31 | async-start | bytes 1310720 | tf_op jit(solution)/shard_map/reduce_scatter | solution.py:251
  374.3 108.1 %reduce-scatter.17.cloned.1.call-start = ((), (), s32[]{:S(2)}) async-start(), calls=%async_computation.28 | async-start | bytes 983040 | tf_op jit(solution)/shard_map/reduce_scatter | solution.py:285
  396.8 3.5 copy-start.1
  407.8 4.6 copy-start.2
  412.4 84.8 %reduce-scatter.19.cloned.1.call-start = ((), (), s32[]{:S(2)}) async-start(), calls=%async_computation.29 | async-start | bytes 327680 | tf_op jit(solution)/shard_map/reduce_scatter | solution.py:298
  422.1 117.7 %reduce-scatter.25.cloned.1.call-start = ((), (), s32[]{:S(2)}) async-start(), calls=%async_computation.32 | async-start | bytes 2359296
  431.8 9.8 %all-to-all-start.4 = ((bf16[128,8,128]{2,0,1:T(8,128)(2,1)}), bf16[128,8,128]{2,0,1:T(8,128)(2,1)S(1)}, u32[]{:S(2)}, u32[]{:S(2)}) async-start(bf16[128,8,128]{2,0,1:T(8,128)(2,1)} %bitcast.218), calls=%async_computation.6 | async-start | bytes 524288 | tf_op jit(solution)/shard_map/all_to_all | solution.py:51
  442.3 12.2 %all-to-all-start.8 = ((bf16[128,4,256]{2,0,1:T(8,128)(2,1)}), bf16[128,4,256]{2,0,1:T(8,128)(2,1)S(1)}, u32[]{:S(2)}, u32[]{:S(2)}) async-start(bf16[128,4,256]{2,0,1:T(8,128)(2,1)} %bitcast.214), calls=%async_computation.14 | async-start | bytes 524288 | tf_op jit(solution)/shard_map/all_to_all | solution.py:349
  454.5 12.8 %all-to-all-start.9 = ((bf16[128,4,256]{2,0,1:T(8,128)(2,1)}), bf16[128,4,256]{2,0,1:T(8,128)(2,1)}, u32[]{:S(2)}, u32[]{:S(2)}) async-start(bf16[128,4,256]{2,0,1:T(8,128)(2,1)} %bitcast.213), calls=%async_computation.16 | async-start | bytes 524288 | tf_op jit(solution)/shard_map/all_to_all | solution.py:350
  466.2 14.3 %copy-start.33 = (f32[128]{0:T(128)S(1)}, f32[128]{0:T(128)}, u32[]{:S(2)}) copy-start(f32[128]{0:T(128)} %param.42) | copy-start | bytes 1540
  466.2 14.3 %copy-start.34 = (f32[128]{0:T(128)S(1)}, f32[128]{0:T(128)}, u32[]{:S(2)}) copy-start(f32[128]{0:T(128)} %param.43) | copy-start | bytes 1540
  466.2 14.3 %copy-start.35 = (f32[128]{0:T(128)S(1)}, f32[128]{0:T(128)}, u32[]{:S(2)}) copy-start(f32[128]{0:T(128)} %param.44) | copy-start | bytes 1540
  466.2 14.9 %copy-start.29 = (f32[2,48]{1,0:T(2,128)S(1)}, f32[2,48]{1,0:T(2,128)}, u32[]{:S(2)}) copy-start(f32[2,48]{1,0:T(2,128)} %param.39) | copy-start | bytes 1156
  466.2 14.9 %copy-start.30 = (f32[2,48]{1,0:T(2,128)S(1)}, f32[2,48]{1,0:T(2,128)}, u32[]{:S(2)}) copy-start(f32[2,48]{1,0:T(2,128)} %param.40) | copy-start | bytes 1156
  466.2 14.9 %copy-start.31 = (f32[2,48]{1,0:T(2,128)S(1)}, f32[2,48]{1,0:T(2,128)}, u32[]{:S(2)}) copy-start(f32[2,48]{1,0:T(2,128)} %param.41) | copy-start | bytes 1156
  466.3 15.4 %copy-start.24 = (f32[6,32]{1,0:T(8,128)S(1)}, f32[6,32]{1,0:T(8,128)}, u32[]{:S(2)}) copy-start(f32[6,32]{1,0:T(8,128)} %param.45) | copy-start | bytes 2308
  466.3 15.4 %copy-start.25 = (f32[6,32]{1,0:T(8,128)S(1)}, f32[6,32]{1,0:T(8,128)}, u32[]{:S(2)}) copy-start(f32[6,32]{1,0:T(8,128)} %param.46) | copy-start | bytes 2308
  466.3 15.4 %copy-start.26 = (f32[6,32]{1,0:T(8,128)S(1)}, f32[6,32]{1,0:T(8,128)}, u32[]{:S(2)}) copy-start(f32[6,32]{1,0:T(8,128)} %param.47) | copy-start | bytes 2308
  466.6 30.6 %copy-start.21 = (f32[128,256]{1,0:T(8,128)S(1)}, f32[128,256]{1,0:T(8,128)}, u32[]{:S(2)}) copy-start(f32[128,256]{1,0:T(8,128)} %param.30) | copy-start | bytes 393220
  466.6 30.6 %copy-start.22 = (f32[128,256]{1,0:T(8,128)S(1)}, f32[128,256]{1,0:T(8,128)}, u32[]{:S(2)}) copy-start(f32[128,256]{1,0:T(8,128)} %param.31) | copy-start | bytes 393220
  467.3 12.9 %all-to-all-start.10 = ((f32[32,1,416]{2,1,0:T(1,128)}), f32[32,1,416]{2,1,0:T(1,128)S(1)}, u32[]{:S(2)}, u32[]{:S(2)}) async-start(f32[32,1,416]{2,1,0:T(1,128)} %copy.165), calls=%async_computation.17 | async-start | bytes 131072 | tf_op jit(solution)/shard_map/all_to_all | solution.py:332
  476.0 23.2 %copy-start.5 = (f32[64,8,3,64]{0,3,2,1:T(8,128)S(1)}, f32[64,8,3,64]{0,3,2,1:T(8,128)}, u32[]{:S(2)}) copy-start(f32[64,8,3,64]{0,3,2,1:T(8,128)} %copy.158) | copy-start | bytes 1179652
  482.3 16.6 %all-to-all-start.6 = ((bf16[4,64,384]{2,1,0:T(8,128)(2,1)}), bf16[4,64,384]{2,1,0:T(8,128)(2,1)S(1)}, u32[]{:S(2)}, u32[]{:S(2)}) async-start(bf16[4,64,384]{2,1,0:T(8,128)(2,1)} %bitcast.232), calls=%async_computation.10 | async-start | bytes 393216 | tf_op jit(solution)/shard_map/all_to_all | solution.py:345
  502.5 4.7 copy-start.6
  504.8 37.0 %copy-start.10 = (bf16[128,8,128]{2,0,1:T(8,128)(2,1)S(1)}, bf16[128,8,128]{2,0,1:T(8,128)(2,1)}, u32[]{:S(2)}) copy-start(bf16[128,8,128]{2,0,1:T(8,128)(2,1)} %copy-done.9) | copy-start | bytes 786436
  (12 other events, 13.3 us)
Sparse Core Ops, SparseCore 0:
  10.8 30.9 all-gather.7
  134.6 40.2 reduce-scatter.10
  242.2 39.5 reduce-scatter.12
  321.3 41.1 reduce-scatter.14
Sparse Core Ops, SparseCore 1:
  144.4 27.9 all-gather.11
  178.2 27.7 all-gather.9
  208.0 30.1 all-gather.13
  284.6 27.7 all-gather.15
  366.1 27.7 all-gather.17
  396.2 27.1 reduce-scatter.20
  425.6 25.7 reduce-scatter.22
  454.1 21.6 reduce-scatter.16
  478.0 19.2 reduce-scatter.18
  500.5 39.3 reduce-scatter.24
